TPU v7x, 256 devices: a whole 4x4x8 slice. The times are simulated.
256 devices in a mesh: section: 32 (over y, x, z_lo), tensor: 8 (over z_hi, core).
Axes of the slice: x: 4, y: 4, z: 8 (z_hi: 4, z_lo: 2; z = z_hi * 2 + z_lo), core: 2. Of those that a mesh axis runs over, the one named last changes fastest.
Arguments:
- layer_inputs: bfloat16 [32, 256, 1536], P('section', 'tensor'), may hold values from -6 to 6
- output_grads: bfloat16 [32, 256, 1536], P('section', 'tensor'), may hold values from -6 to 6
- held_inputs: bfloat16 [32, 2, 256, 1536], P('section', None, 'tensor'), may hold values from -6 to 6
- held_qkv: bfloat16 [32, 3, 256, 1536], P('section', None, None, 'tensor'), may hold values from -120 to 120
- held_gateup: bfloat16 [32, 2, 256, 3072], P('section', None, None, 'tensor'), may hold values from -6 to 6
- swapped_pairs: int32 [16], replicated, may hold values 0 or 1
- w_qkv: bfloat16 [32, 3, 1536, 1536], P('section', None, None, 'tensor'), may hold values from -14 to 14
- w_out: bfloat16 [32, 1536, 1536], P('section', 'tensor'), may hold values from -0.15625 to 0.15625
- w_gateup: bfloat16 [32, 2, 1536, 3072], P('section', None, None, 'tensor'), may hold values from -0.15625 to 0.15625
- w_down: bfloat16 [32, 3072, 1536], P('section', 'tensor'), may hold values from -0.109375 to 0.109375
- norm_gains: float32 [32, 2, 1536], P('section'), may hold values from 0.5 to 1.5
Outputs:
- forward_sent: bfloat16 [32, 256, 1536], P('section', 'tensor')
- backward_sent: bfloat16 [32, 256, 1536], P('section', 'tensor')
- stash_inputs: bfloat16 [32, 2, 256, 1536], P('section', None, 'tensor')
- stash_qkv: bfloat16 [32, 3, 256, 1536], P('section', None, None, 'tensor')
- stash_gateup: bfloat16 [32, 2, 256, 3072], P('section', None, None, 'tensor')
- grad_qkv: bfloat16 [32, 3, 1536, 1536], P('section', None, None, 'tensor')
- grad_out: bfloat16 [32, 1536, 1536], P('section', 'tensor')
- grad_gateup: bfloat16 [32, 2, 1536, 3072], P('section', None, None, 'tensor')
- grad_down: bfloat16 [32, 3072, 1536], P('section', 'tensor')
- grad_gains: float32 [32, 2, 1536], P('section')
Inputs may be any that keep to these rules, and one draw needn't show every extreme that they name: `swapped_pairs`: 1 marks a pair of sections i and 31 - i whose stashes each sit on the other device of the pair.
All inputs are finite; a program needn't handle non-finite values.
Results may differ from a plain program's by a relative error of at most 0.023.
Values may be sent and summed in bfloat16 or wider, within the bound.
No kernel may reach another device: no remote copies, remote signals or barrier semaphores. Data moves between devices by JAX's collectives and lax.ppermute only.
A program may use at most 128 MiB of HBM per device.

v0:
```python
import math

import jax
import jax.numpy as jnp
from jax import lax
from jax.experimental import pallas as pl
from jax.experimental.pallas import tpu as pltpu
from jax.sharding import PartitionSpec as P

D = 1536
HEADS = 16
HEAD = D // HEADS
EPSILON = 1e-05
BF = jnp.bfloat16
F32 = jnp.float32
NN = ((1,), (0,))
NT = ((1,), (1,))
TN = ((0,), (0,))
VMEM = 16 * 2**20


def dot(a, b, dims):
    return lax.dot_general(a, b, (dims, ((), ())), preferred_element_type=F32)


def tensor_pairs(step_even, step_odd):
    return [
        (t, ((t // 2 + (step_odd if t % 2 else step_even)) % 4) * 2 + t % 2) for t in range(8)
    ]


CORE = [(t, t ^ 1) for t in range(8)]
GATHER = tensor_pairs(1, -1)
REDUCE = tensor_pairs(-1, 1)


def over(value, pairs):
    return lax.ppermute(value, "tensor", pairs)


def after(value, *earlier):
    return lax.optimization_barrier((value, *earlier))[0] if earlier else value


def add(one, other):
    return (one.astype(F32) + other.astype(F32)).astype(BF)


def gather(own):
    near_0, other = over(own, GATHER), over(own, CORE)
    near_1, far = over(other, GATHER), over(near_0, GATHER)
    s_1 = over(near_1, CORE)
    return own, other, near_0, near_1, far, over(near_0, CORE), s_1, over(after(far, s_1), CORE)


def reduce_blocks(parts):
    held_2 = add(parts[4], over(parts[7], CORE))
    far = over(held_2, REDUCE)
    held_1 = add(parts[3], over(parts[6], CORE))
    near_1 = over(held_1, REDUCE)
    held_0 = add(add(parts[2], over(parts[5], CORE)), far)
    near_0 = over(held_0, REDUCE)
    other = add(parts[1], near_1)
    return (parts[0], near_0, over(other, CORE)), other


def all_sum(value):
    for pairs in (CORE, [(t, t ^ 2) for t in range(8)], [(t, t ^ 4) for t in range(8)]):
        value = value + over(value, pairs)
    return value


def call(body, name, outs, scratch, flops, args, streamed=()):
    smem, vmem = pl.BlockSpec(memory_space=pltpu.SMEM), pl.BlockSpec(memory_space=pltpu.VMEM)
    hbm = pl.BlockSpec(memory_space=pltpu.HBM)
    args = [
        pltpu.with_memory_space_constraint(a, pltpu.HBM) if i in streamed else a
        for i, a in enumerate(args)
    ]
    moved = sum(a.size * a.dtype.itemsize for a in args)
    moved += sum(math.prod(o.shape) * o.dtype.itemsize for o in outs)
    return pl.pallas_call(
        body,
        name=name,
        out_shape=outs,
        in_specs=[
            hbm if i in streamed else smem if a.dtype == jnp.int32 else vmem
            for i, a in enumerate(args)
        ],
        out_specs=[vmem] * len(outs),
        scratch_shapes=scratch,
        cost_estimate=pl.CostEstimate(flops=flops, bytes_accessed=moved, transcendentals=0),
        compiler_params=pltpu.CompilerParams(vmem_limit_bytes=VMEM),
    )(*args)


def shape(*dims, dtype=BF):
    return jax.ShapeDtypeStruct(dims, dtype)


def block_rows():
    place = lax.axis_index("tensor")
    chip, core = place // 2, place % 2
    step = 2 * core - 1
    where = (
        (0, core), (0, 1 - core), (step, core), (step, 1 - core),
        (2, core), (-step, 1 - core), (-step, core), (2, 1 - core),
    )
    starts = [(((chip + dz + 4) % 4) * 2 + c) * 32 for dz, c in where]
    return [pl.ds(pl.multiple_of(start, 32), 32) for start in starts]


def moved_stash(flags):
    position = lax.axis_index("section")
    return flags[jnp.minimum(position, lax.axis_size("section") - 1 - position)] > 0


def unit_scale(values):
    return lax.rsqrt(jnp.mean(values * values, axis=-1, keepdims=True) + EPSILON)


def row_norm(block, gain):
    values = block.astype(F32)
    return values * unit_scale(values) * gain


def fill(full, rows, blocks, which, change=None):
    for place, block in zip(rows, blocks):
        full[place, :] = block[which] if change is None else change(block[which])


def spread(total, rows, parts, which):
    for place, part in zip(rows, parts):
        part[which] = total[place, :].astype(BF)


SPREAD = [shape(2, 32, D)] * 8


PARTS = ((2, 32, D), (3, 192, 256))
STASH = sum(math.prod(part) for part in PARTS) // 128


def stash_blocks():
    start = 0
    for part, (count, length, width) in enumerate(PARTS):
        for column in range(0, width, 128):
            for index in range(count):
                yield part, index, pl.ds(column, 128), pl.ds(start, length)
                start += length


def pack_stash(parts, packed):
    for part, index, columns, rows in stash_blocks():
        packed[rows, :] = parts[part][index, :, columns]


def pick_stash(moved, packed, kept, outs):
    for part, index, columns, rows in stash_blocks():
        if outs[part] is not None:
            outs[part][index, :, columns] = jnp.where(
                moved, packed[rows, :], kept[part][index, :, columns]
            )


def pack_held(x, q, packed):
    pack_stash((x, q), packed)


def pack_new(x, mids, qkv, packed, pair):
    pair[0] = x[...]
    pair[1] = mids[0]
    pack_stash((pair, qkv), packed)


def stash_out(flags, packed, x, mids, qkv, out_x, out_qkv, pair):
    pair[0] = x[...]
    pair[1] = mids[0]
    pick_stash(moved_stash(flags), packed, (pair, qkv), (out_x, out_qkv))


def stash_out_last(flags, moved, kept, out):
    out[...] = jnp.where(moved_stash(flags), moved[...], kept[...])


def probs_of(keys, queries):
    scores = dot(keys, queries, TN) * HEAD ** (-0.5)
    length = scores.shape[0]
    key = lax.broadcasted_iota(jnp.int32, (length, length), 0)
    query = lax.broadcasted_iota(jnp.int32, (length, length), 1)
    scores = jnp.where(key <= query, scores, -1e30)
    powers = jnp.exp(scores - jnp.max(scores, axis=0, keepdims=True))
    return powers / jnp.sum(powers, axis=0, keepdims=True)


def bring(*refs):
    count = len(refs) // 3
    copies = [
        pltpu.make_async_copy(*each)
        for each in zip(refs[:count], refs[count : 2 * count], refs[2 * count :])
    ]
    for copy in copies:
        copy.start()
    for copy in copies:
        copy.wait()


def forward_attention(gains, wqkv, wout, qkv, full, mixed, total):
    for c in range(3):
        qkv[c] = dot(wqkv[c], full[...], NT).astype(BF)
    for h in range(2):
        rows = pl.ds(h * HEAD, HEAD)
        probs = probs_of(qkv[1, rows, :], qkv[0, rows, :]).astype(BF)
        mixed[rows, :] = dot(qkv[2, rows, :], probs, NN).astype(BF)
    total[...] = dot(mixed[...], wout[...], TN)


def forward_mlp(wgateup, wdown, gateup, full, total):
    for c in range(2):
        gateup[c] = dot(full[...], wgateup[c], NN).astype(BF)
    gate = gateup[0].astype(F32)
    act = (gate * jax.nn.sigmoid(gate) * gateup[1].astype(F32)).astype(BF)
    total[...] = dot(act, wdown[...], NN)


def backward_mlp(stash, wgateup, wdown, dgateup, act_low, grads, total):
    gate = stash[0].astype(F32)
    up = stash[1].astype(F32)
    sig = jax.nn.sigmoid(gate)
    silu = gate * sig
    act_low[...] = (silu * up).astype(BF)
    dact = dot(grads[...], wdown[...], NT)
    dgateup[0] = (dact * up * sig * (1.0 + gate * (1.0 - sig))).astype(BF)
    dgateup[1] = (dact * silu).astype(BF)
    total[...] = dot(dgateup[0], wgateup[0], NT) + dot(dgateup[1], wgateup[1], NT)


def backward_attention(qkv, probs, wqkv, wout, dqkv, dmid, dmixed, total):
    dmixed[...] = dot(wout[...], dmid[...], NT).astype(BF)
    for h in range(2):
        rows = pl.ds(h * HEAD, HEAD)
        out = dmixed[rows, :]
        weight = probs[h]
        dqkv[2, rows, :] = dot(out, weight.astype(BF), NT).astype(BF)
        dprob = dot(qkv[2, rows, :], out, TN)
        inner = jnp.sum(dprob * weight, axis=0, keepdims=True)
        dscore = (weight * (dprob - inner) * HEAD ** (-0.5)).astype(BF)
        dqkv[0, rows, :] = dot(qkv[1, rows, :], dscore, NN).astype(BF)
        dqkv[1, rows, :] = dot(qkv[0, rows, :], dscore, NT).astype(BF)
    total[...] = dot(dqkv[0], wqkv[0], TN) + dot(dqkv[1], wqkv[1], TN) + dot(dqkv[2], wqkv[2], TN)


def first_stage(
    flags, own_b, other, near_0, near_1, far, s_0, s_1, s_2, gains, fetched, wqkv, wout, held, wdown, wgateup,
    qkv, dgateup, act_low, grads, p_0, p_1, p_2, p_3, p_4, p_5, p_6, p_7, full, mixed, total, stash,
):
    parts = (p_0, p_1, p_2, p_3, p_4, p_5, p_6, p_7)
    rows, blocks, gain = block_rows(), (own_b, other, near_0, near_1, far, s_0, s_1, s_2), gains[0:1, :]
    fill(full, rows, blocks, 0, lambda part: row_norm(part, gain).astype(BF))
    forward_attention(gains, wqkv, wout, qkv, full, mixed, total)
    spread(total, rows, parts, 0)
    fill(grads, rows, blocks, 1)
    stash[...] = jnp.where(moved_stash(flags), fetched[...], held[...])
    backward_mlp(stash, wgateup, wdown, dgateup, act_low, grads, total)
    spread(total, rows, parts, 1)


def second_stage(
    own_b, other, near_0, near_1, far, s_0, s_1, s_2, gains, stash_q, probs, wgateup, wdown, wout, wqkv,
    gateup, dqkv, dmid, p_0, p_1, p_2, p_3, p_4, p_5, p_6, p_7, full, dmixed, total,
):
    parts = (p_0, p_1, p_2, p_3, p_4, p_5, p_6, p_7)
    rows, blocks, gain = block_rows(), (own_b, other, near_0, near_1, far, s_0, s_1, s_2), gains[1:2, :]
    fill(full, rows, blocks, 0, lambda part: row_norm(part, gain).astype(BF))
    forward_mlp(wgateup, wdown, gateup, full, total)
    spread(total, rows, parts, 0)
    fill(dmid, rows, blocks, 1)
    backward_attention(stash_q, probs, wqkv, wout, dqkv, dmid, dmixed, total)
    spread(total, rows, parts, 1)


def backward_probs(flags, held, fetched, qkv, mixed, probs):
    pick_stash(moved_stash(flags), fetched, (None, held), (None, qkv))
    for h in range(2):
        rows = pl.ds(h * HEAD, HEAD)
        probs[h] = probs_of(qkv[1, rows, :], qkv[0, rows, :])
        mixed[rows, :] = dot(qkv[2, rows, :], probs[h].astype(BF), NN).astype(BF)


def mlp_weights(own_b, other, near_0, near_1, far, s_0, s_1, s_2, gains, dgateup, act_low, grads, grad_gateup, grad_down, full):
    gain = gains[1:2, :]
    grad_down[...] = dot(act_low[...], grads[...], TN).astype(BF)
    fill(full, block_rows(), (own_b, other, near_0, near_1, far, s_0, s_1, s_2), 3, lambda part: row_norm(part, gain).astype(BF))
    for c in range(2):
        grad_gateup[c] = dot(full[...], dgateup[c], TN).astype(BF)


def attention_weights(
    own_b, other, near_0, near_1, far, s_0, s_1, s_2, gains, dqkv, mixed, dmid, wqkv, grad_qkv, grad_out, gain_terms, full,
):
    gain = gains[0:1, :]
    grad_out[...] = dot(mixed[...], dmid[...], NN).astype(BF)
    fill(full, block_rows(), (own_b, other, near_0, near_1, far, s_0, s_1, s_2), 2, lambda part: row_norm(part, gain).astype(BF))
    terms = jnp.zeros((1, D), F32)
    for c in range(3):
        grad = dot(dqkv[c], full[...], NN)
        grad_qkv[c] = grad.astype(BF)
        terms += jnp.sum(grad * wqkv[c].astype(F32), axis=0, keepdims=True)
    gain_terms[...] = terms / gain


def total_of(own, near, second, which):
    return own[which].astype(F32) + near[which].astype(F32) + second[which].astype(F32)


def norm_back(source, gain, upstream):
    values = source.astype(F32)
    inverse = unit_scale(values)
    normal = values * inverse
    scaled = upstream * gain
    inner = jnp.mean(scaled * normal, axis=-1, keepdims=True)
    return inverse * (scaled - normal * inner), upstream * normal


def middle(flags, held, fetched, x, dy, own, near, second, gains, out, terms, stash):
    pick_stash(moved_stash(flags), fetched, (held, None), (stash, None))
    out[0] = (x[...].astype(F32) + total_of(own, near, second, 0)).astype(BF)
    back, products = norm_back(stash[1], gains[1:2, :], total_of(own, near, second, 1))
    out[1] = (dy[...].astype(F32) + back).astype(BF)
    out[2] = stash[0]
    out[3] = stash[1]
    terms[...] = jnp.sum(products, axis=0, keepdims=True)


def last(mids, own, near, second, gains, layer_out, dinput):
    layer_out[...] = (mids[0].astype(F32) + total_of(own, near, second, 0)).astype(BF)
    back, _ = norm_back(mids[2], gains[0:1, :], total_of(own, near, second, 1))
    dinput[...] = (mids[1].astype(F32) + back).astype(BF)


def shifted(value, by):
    count = lax.axis_size("section")
    pairs = [(i, i + by) for i in range(count) if 0 <= i + by < count]
    return lax.ppermute(value, "section", pairs)


def mirrored(value):
    count = lax.axis_size("section")
    return lax.ppermute(value, "section", [(i, count - 1 - i) for i in range(count)])


def on_device(
    layer_inputs, output_grads, held_inputs, held_qkv, held_gateup, swapped_pairs,
    w_qkv, w_out, w_gateup, w_down, norm_gains,
):
    layer_in, dy = layer_inputs[0], output_grads[0]
    wqkv = jnp.swapaxes(w_qkv[0], 1, 2)
    held_q = jnp.swapaxes(held_qkv[0], 1, 2)
    wout, wgateup, wdown, gains = w_out[0], w_gateup[0], w_down[0], norm_gains[0]
    held_x, held_g = held_inputs[0], held_gateup[0]
    mega = 256 * 1536 * 2
    full, total = pltpu.VMEM((256, D), BF), pltpu.VMEM((256, D), F32)
    per_head, pair = pltpu.VMEM((192, 256), BF), pltpu.VMEM((2, 32, D), BF)

    blocks = gather(jnp.stack([layer_in, dy]))
    fetched_g = mirrored(after(held_g, blocks[3]))
    (packed,) = call(pack_held, "pack_held", [shape(STASH, 128)], [], 1024, (held_x, held_q))
    fetched = mirrored(after(packed, blocks[4]))
    weights = [after(wqkv, blocks[1]), wout, held_g, wdown, wgateup]
    wqkv, wout, held_g, wdown, wgateup = call(
        bring, "bring", [pltpu.VMEM(w.shape, w.dtype) for w in weights],
        [pltpu.SemaphoreType.DMA(()) for _ in weights], 0, weights, (0, 1, 2, 3, 4),
    )

    qkv, dgateup, act_low, grads, *parts = call(
        first_stage, "first_stage",
        [shape(3, 192, 256), shape(2, 256, 384), shape(256, 384), shape(256, D)] + SPREAD,
        [full, per_head, total, pltpu.VMEM((2, 256, 384), BF)],
        mega * 2050,
        (swapped_pairs, *blocks, gains, fetched_g, wqkv, wout, held_g, wdown, wgateup),
    )
    parts[7] = after(parts[7], fetched)
    sums, _ = reduce_blocks(parts)
    mids, mid_terms = call(
        middle, "middle", [shape(4, 32, D), shape(1, D, dtype=F32)], [pair],
        32 * D * 40, (swapped_pairs, held_x, fetched, layer_in, dy, *sums, gains),
    )

    stash_q, mixed, probs = call(
        backward_probs, "backward_probs",
        [shape(3, 192, 256), shape(192, 256), shape(2, 256, 256, dtype=F32)], [],
        mega * 128, (swapped_pairs, held_q, fetched),
    )
    blocks = gather(mids)
    (packed,) = call(pack_new, "pack_new", [shape(STASH, 128)], [pair], 1024, (layer_in, mids, qkv))
    moved = mirrored(after(packed, blocks[2]))

    gateup, dqkv, dmid, *parts = call(
        second_stage, "second_stage",
        [shape(2, 256, 384), shape(3, 192, 256), shape(256, D)] + SPREAD,
        [full, per_head, total],
        mega * 2150,
        (*blocks, gains, stash_q, probs, wgateup, wdown, wout, wqkv),
    )
    parts[7] = after(parts[7], moved)
    sums, other = reduce_blocks(parts)
    moved_gateup = mirrored(after(gateup, other))

    grad_qkv, grad_out, in_terms = call(
        attention_weights, "attention_weights",
        [shape(3, 192, D), shape(192, D), shape(1, D, dtype=F32)], [full],
        mega * 768, (*blocks, gains, dqkv, mixed, dmid, wqkv),
    )
    grad_gateup, grad_down = call(
        mlp_weights, "mlp_weights",
        [shape(2, D, 384), shape(384, D)], [full],
        mega * 1152, (*blocks, gains, dgateup, act_low, after(grads, gateup)),
    )
    layer_out, dinput = call(
        last, "last", [shape(32, D), shape(32, D)], [],
        32 * D * 40, (after(mids, grad_down, in_terms), *sums, gains),
    )
    forward_sent = shifted(layer_out, 1)
    backward_sent = shifted(dinput, -1)
    grad_gains = all_sum(jnp.concatenate([in_terms, mid_terms]))

    stash_inputs, stash_qkv = call(
        stash_out, "stash_out", [shape(*part) for part in PARTS], [pair],
        1024, (swapped_pairs, moved, layer_in, mids, qkv),
    )
    (stash_gateup,) = call(
        stash_out_last, "stash_out_last", [shape(2, 256, 384)], [],
        1024, (swapped_pairs, moved_gateup, gateup),
    )
    return (
        forward_sent[None],
        backward_sent[None],
        stash_inputs[None],
        jnp.swapaxes(stash_qkv, 1, 2)[None],
        stash_gateup[None],
        jnp.swapaxes(grad_qkv, 1, 2)[None],
        grad_out[None],
        grad_gateup[None],
        grad_down[None],
        grad_gains[None],
    )


def solution(mesh):
    in_specs = (
        P("section", "tensor", None),
        P("section", "tensor", None),
        P("section", None, "tensor", None),
        P("section", None, None, "tensor"),
        P("section", None, None, "tensor"),
        P(),
        P("section", None, None, "tensor"),
        P("section", "tensor", None),
        P("section", None, None, "tensor"),
        P("section", "tensor", None),
        P("section", None, None),
    )
    out_specs = (
        P("section", "tensor", None),
        P("section", "tensor", None),
        P("section", None, "tensor", None),
        P("section", None, None, "tensor"),
        P("section", None, None, "tensor"),
        P("section", None, None, "tensor"),
        P("section", "tensor", None),
        P("section", None, None, "tensor"),
        P("section", "tensor", None),
        P("section", None, None),
    )
    return jax.shard_map(
        on_device, mesh=mesh, in_specs=in_specs, out_specs=out_specs, check_vma=False
    )
```

profile of v0, /device:TPU:1, one launch (start us, length us, event | category | flops | bytes accessed | tf_op | source)
XLA Modules:
  0.0 160.2 jit_solution(8942193067249294571)
XLA Ops:
  2.4 3.2 %collective-permute-start.3 = (bf16[2,32,1536]{2,1,0:T(8,128)(2,1)S(1)}, bf16[2,32,1536]{2,1,0:T(8,128)(2,1)S(1)}, u32[]{:S(2)}, u32[]{:S(2)}) collective-permute-start(bf16[2,32,1536]{2,1,0:T(8,128)(2,1)S(1)} %constant_dynamic-update-slice_fusion.own_b), channel_id=1, source_target_pairs={{0,1},{1,0},{2,3},{3,2},{4,5},{5,4},{6,7},{7,6},{8,9},{9,8},{10,11... | collective-permute-start | bytes 589832 | tf_op jit(solution)/shard_map/ppermute | solution.py:38
  5.7 4.3 %collective-permute-start = (bf16[2,32,1536]{2,1,0:T(8,128)(2,1)S(1)}, bf16[2,32,1536]{2,1,0:T(8,128)(2,1)S(1)}, u32[]{:S(2)}, u32[]{:S(2)}) collective-permute-start(bf16[2,32,1536]{2,1,0:T(8,128)(2,1)S(1)} %constant_dynamic-update-slice_fusion.own_b), channel_id=1, source_target_pairs={{0,2},{1,7},{2,4},{3,1},{4,6},{5,3},{6,0},{7,5},{8,10},{9,15},{10,... | collective-permute-start | bytes 589832 | tf_op jit(solution)/shard_map/ppermute | solution.py:38
  11.1 2.4 %collective-permute-done.near_0 = bf16[2,32,1536]{2,1,0:T(8,128)(2,1)S(1)} collective-permute-done((bf16[2,32,1536]{2,1,0:T(8,128)(2,1)S(1)}, bf16[2,32,1536]{2,1,0:T(8,128)(2,1)S(1)}, u32[]{:S(2)}, u32[]{:S(2)}) %collective-permute-start) | collective-permute-done | bytes 196640 | tf_op jit(solution)/shard_map/ppermute | solution.py:38
  13.5 3.2 %collective-permute-start.1 = (bf16[2,32,1536]{2,1,0:T(8,128)(2,1)S(1)}, bf16[2,32,1536]{2,1,0:T(8,128)(2,1)S(1)}, u32[]{:S(2)}, u32[]{:S(2)}) collective-permute-start(bf16[2,32,1536]{2,1,0:T(8,128)(2,1)S(1)} %collective-permute-done.near_0), channel_id=1, source_target_pairs={{0,2},{1,7},{2,4},{3,1},{4,6},{5,3},{6,0},{7,5},{8,10},{9,15},{10,... | collective-permute-start | bytes 589832 | tf_op jit(solution)/shard_map/ppermute | solution.py:38
  17.7 2.1 %collective-permute-start.6 = (bf16[2,32,1536]{2,1,0:T(8,128)(2,1)S(1)}, bf16[2,32,1536]{2,1,0:T(8,128)(2,1)S(1)}, u32[]{:S(2)}, u32[]{:S(2)}) collective-permute-start(bf16[2,32,1536]{2,1,0:T(8,128)(2,1)S(1)} %collective-permute-done.4.near_1), channel_id=1, source_target_pairs={{0,1},{1,0},{2,3},{3,2},{4,5},{5,4},{6,7},{7,6},{8,9},{9,8},{10,11... | collective-permute-start | bytes 589832 | tf_op jit(solution)/shard_map/ppermute | solution.py:38
  19.8 5.9 %collective-permute-start.8 = (bf16[2,256,384]{2,1,0:T(8,128)(2,1)}, bf16[2,256,384]{2,1,0:T(8,128)(2,1)S(1)}, u32[]{:S(2)}, u32[]{:S(2)}) collective-permute-start(bf16[2,256,384]{2,1,0:T(8,128)(2,1)} %bitcast.47), channel_id=1, source_target_pairs={{0,248},{8,240},{16,232},{24,224},{32,216},{40,208},{48,200},{56,1... | collective-permute-start | bytes 1179656 | tf_op jit(solution)/shard_map/ppermute | solution.py:349
  28.2 4.8 %collective-permute-start.2 = (bf16[1920,128]{1,0:T(8,128)(2,1)S(1)}, bf16[1920,128]{1,0:T(8,128)(2,1)S(1)}, u32[]{:S(2)}, u32[]{:S(2)}) collective-permute-start(bf16[1920,128]{1,0:T(8,128)(2,1)S(1)} %pack_held.1), channel_id=1, source_target_pairs={{0,248},{8,240},{16,232},{24,224},{32,216},{40,208},{48,200},{56,1... | collective-permute-start | bytes 1474568 | tf_op jit(solution)/shard_map/ppermute | solution.py:349
  33.0 2.9 %bring.1 = (bf16[3,192,1536]{2,1,0:T(8,128)(2,1)S(1)}, bf16[192,1536]{1,0:T(8,128)(2,1)S(1)}, bf16[2,256,384]{2,1,0:T(8,128)(2,1)S(1)}, bf16[384,1536]{1,0:T(8,128)(2,1)S(1)}, bf16[2,1536,384]{2,1,0:T(8,128)(2,1)S(1)}) custom-call(bf16[3,192,1536]{2,1,0:T(8,128)(2,1)} %bitcast.44, bf16[192,1536]{1,0:T(8,128)(2,1)} %bitcast.46, ...), custom_call_target="tpu_custom_call" | custom-call | bytes 12582912 | tf_op jit(solution)/shard_map/bring/pallas_call | solution.py:82
  36.1 4.6 %first_stage.1 = (bf16[3,192,256]{2,1,0:T(8,128)(2,1)S(1)}, bf16[2,256,384]{2,1,0:T(8,128)(2,1)S(1)}, bf16[256,384]{1,0:T(8,128)(2,1)S(1)}, bf16[256,1536]{1,0:T...) custom-call(s32[16]{0:T(128)S(1)} %copy-done.6, ...), custom_call_target="tpu_custom_call" | custom-call | flops 1612185600 | bytes 11513920 | tf_op jit(solution)/shard_map/first_stage/pallas_call | solution.py:82
  41.3 5.2 %collective-permute-done.2.fetched = bf16[1920,128]{1,0:T(8,128)(2,1)S(1)} collective-permute-done((bf16[1920,128]{1,0:T(8,128)(2,1)S(1)}, bf16[1920,128]{1,0:T(8,128)(2,1)S(1)}, u32[]{:S(2)}, u32[]{:S(2)}) %collective-permute-start.2) | collective-permute-done | bytes 491552 | tf_op jit(solution)/shard_map/ppermute | solution.py:349
  47.0 3.0 %collective-permute-start.14 = (bf16[2,32,1536]{2,1,0:T(8,128)(2,1)S(1)}, bf16[2,32,1536]{2,1,0:T(8,128)(2,1)S(1)}, u32[]{:S(2)}, u32[]{:S(2)}) collective-permute-start(bf16[2,32,1536]{2,1,0:T(8,128)(2,1)S(1)} %add_convert_fusion.6), channel_id=1, source_target_pairs={{0,6},{1,3},{2,0},{3,5},{4,2},{5,7},{6,4},{7,1},{8,14},{9,11},{10,... | collective-permute-start | bytes 589832 | tf_op jit(solution)/shard_map/ppermute | solution.py:38
  50.1 3.6 %collective-permute-start.11 = (bf16[2,32,1536]{2,1,0:T(8,128)(2,1)S(1)}, bf16[2,32,1536]{2,1,0:T(8,128)(2,1)S(1)}, u32[]{:S(2)}, u32[]{:S(2)}) collective-permute-start(bf16[2,32,1536]{2,1,0:T(8,128)(2,1)S(1)} %add_convert_fusion.8), channel_id=1, source_target_pairs={{0,6},{1,3},{2,0},{3,5},{4,2},{5,7},{6,4},{7,1},{8,14},{9,11},{10,... | collective-permute-start | bytes 589832 | tf_op jit(solution)/shard_map/ppermute | solution.py:38
  58.2 4.5 %collective-permute-start.12 = (bf16[2,32,1536]{2,1,0:T(8,128)(2,1)S(1)}, bf16[2,32,1536]{2,1,0:T(8,128)(2,1)S(1)}, u32[]{:S(2)}, u32[]{:S(2)}) collective-permute-start(bf16[2,32,1536]{2,1,0:T(8,128)(2,1)S(1)} %add_convert_fusion.7), channel_id=1, source_target_pairs={{0,6},{1,3},{2,0},{3,5},{4,2},{5,7},{6,4},{7,1},{8,14},{9,11},{10,... | collective-permute-start | bytes 589832 | tf_op jit(solution)/shard_map/ppermute | solution.py:38
  62.7 4.8 %collective-permute-done.12.near = bf16[2,32,1536]{2,1,0:T(8,128)(2,1)S(1)} collective-permute-done((bf16[2,32,1536]{2,1,0:T(8,128)(2,1)S(1)}, bf16[2,32,1536]{2,1,0:T(8,128)(2,1)S(1)}, u32[]{:S(2)}, u32[]{:S(2)}) %collective-permute-start.12) | collective-permute-done | bytes 196640 | tf_op jit(solution)/shard_map/ppermute | solution.py:38
  68.3 3.5 %collective-permute-start.16 = (bf16[4,32,1536]{2,1,0:T(8,128)(2,1)S(1)}, bf16[4,32,1536]{2,1,0:T(8,128)(2,1)S(1)}, u32[]{:S(2)}, u32[]{:S(2)}) collective-permute-start(bf16[4,32,1536]{2,1,0:T(8,128)(2,1)S(1)} %get-tuple-element.95.own_b.mids), channel_id=1, source_target_pairs={{0,1},{1,0},{2,3},{3,2},{4,5},{5,4},{6,7},{7,6},{8,9},{9,8},{10,11... | collective-permute-start | bytes 1179656 | tf_op jit(solution)/shard_map/ppermute | solution.py:38
  71.9 4.3 %collective-permute-start.17 = (bf16[4,32,1536]{2,1,0:T(8,128)(2,1)S(1)}, bf16[4,32,1536]{2,1,0:T(8,128)(2,1)S(1)}, u32[]{:S(2)}, u32[]{:S(2)}) collective-permute-start(bf16[4,32,1536]{2,1,0:T(8,128)(2,1)S(1)} %get-tuple-element.95.own_b.mids), channel_id=1, source_target_pairs={{0,2},{1,7},{2,4},{3,1},{4,6},{5,3},{6,0},{7,5},{8,10},{9,15},{10,... | collective-permute-start | bytes 1179656 | tf_op jit(solution)/shard_map/ppermute | solution.py:38
  77.5 5.8 %collective-permute-done.17.near_0 = bf16[4,32,1536]{2,1,0:T(8,128)(2,1)S(1)} collective-permute-done((bf16[4,32,1536]{2,1,0:T(8,128)(2,1)S(1)}, bf16[4,32,1536]{2,1,0:T(8,128)(2,1)S(1)}, u32[]{:S(2)}, u32[]{:S(2)}) %collective-permute-start.17) | collective-permute-done | bytes 393248 | tf_op jit(solution)/shard_map/ppermute | solution.py:38
  83.3 4.0 %collective-permute-start.19 = (bf16[4,32,1536]{2,1,0:T(8,128)(2,1)S(1)}, bf16[4,32,1536]{2,1,0:T(8,128)(2,1)S(1)}, u32[]{:S(2)}, u32[]{:S(2)}) collective-permute-start(bf16[4,32,1536]{2,1,0:T(8,128)(2,1)S(1)} %collective-permute-done.17.near_0), channel_id=1, source_target_pairs={{0,2},{1,7},{2,4},{3,1},{4,6},{5,3},{6,0},{7,5},{8,10},{9,15},{10,... | collective-permute-start | bytes 1179656 | tf_op jit(solution)/shard_map/ppermute | solution.py:38
  87.3 2.5 %collective-permute-done.18.near_1 = bf16[4,32,1536]{2,1,0:T(8,128)(2,1)S(1)} collective-permute-done((bf16[4,32,1536]{2,1,0:T(8,128)(2,1)S(1)}, bf16[4,32,1536]{2,1,0:T(8,128)(2,1)S(1)}, u32[]{:S(2)}, u32[]{:S(2)}) %collective-permute-start.18) | collective-permute-done | bytes 393248 | tf_op jit(solution)/shard_map/ppermute | solution.py:38
  89.8 8.8 %collective-permute-start.21 = (bf16[4,32,1536]{2,1,0:T(8,128)(2,1)S(1)}, bf16[4,32,1536]{2,1,0:T(8,128)(2,1)S(1)}, u32[]{:S(2)}, u32[]{:S(2)}) collective-permute-start(bf16[4,32,1536]{2,1,0:T(8,128)(2,1)S(1)} %collective-permute-done.18.near_1), channel_id=1, source_target_pairs={{0,1},{1,0},{2,3},{3,2},{4,5},{5,4},{6,7},{7,6},{8,9},{9,8},{10,11... | collective-permute-start | bytes 1179656 | tf_op jit(solution)/shard_map/ppermute | solution.py:38
  98.7 2.9 %collective-permute-done.19.far = bf16[4,32,1536]{2,1,0:T(8,128)(2,1)S(1)} collective-permute-done((bf16[4,32,1536]{2,1,0:T(8,128)(2,1)S(1)}, bf16[4,32,1536]{2,1,0:T(8,128)(2,1)S(1)}, u32[]{:S(2)}, u32[]{:S(2)}) %collective-permute-start.19) | collective-permute-done | bytes 393248 | tf_op jit(solution)/shard_map/ppermute | solution.py:38
  104.5 4.1 %second_stage.1 = (bf16[2,256,384]{2,1,0:T(8,128)(2,1)S(1)}, bf16[3,192,256]{2,1,0:T(8,128)(2,1)S(1)}, bf16[256,1536]{1,0:T(8,128)(2,1)S(1)}, bf16[2,32,1536]{2,...) custom-call(bf16[4,32,1536]{2,1,0:T(8,128)(2,1)S(1)} %get-tuple-elem, ...), custom_call_target="tpu_custom_call" | custom-call | flops 1690828800 | bytes 12922880 | tf_op jit(solution)/shard_map/second_stage/pallas_call | solution.py:82
  108.6 2.3 %attention_weights.1 = (bf16[3,192,1536]{2,1,0:T(8,128)(2,1)}, bf16[192,1536]{1,0:T(8,128)(2,1)}, f32[1,1536]{1,0:T(1,128)S(1)}) custom-call(bf16[4,32,1536]{2,1,0:T(8,128)(2,1)S(1)} %get-tuple-element.95.own_b.mids, bf16[4,32,1536]{2,1,0:T(8,128)(2,1)S(1)} %collective-permute-done.16.other, bf16[4,32,1536]{2,1,0:T(8,128)(2,1)S(1)} %collective-permute-done.17.near_0, ...), custom_call_target="tpu_custom_call" | custom-call | flops 603979776 | bytes 8472576 | tf_op jit(solution)/shard_map/attention_weights/pallas_call | solution.py:82
  111.1 9.0 %collective-permute-done.24.packed = bf16[1920,128]{1,0:T(8,128)(2,1)S(1)} collective-permute-done((bf16[1920,128]{1,0:T(8,128)(2,1)S(1)}, bf16[1920,128]{1,0:T(8,128)(2,1)S(1)}, u32[]{:S(2)}, u32[]{:S(2)}) %collective-permute-start.24) | collective-permute-done | bytes 491552 | tf_op jit(solution)/shard_map/ppermute | solution.py:349
  125.6 2.8 %collective-permute-start.26 = (bf16[2,32,1536]{2,1,0:T(8,128)(2,1)S(1)}, bf16[2,32,1536]{2,1,0:T(8,128)(2,1)S(1)}, u32[]{:S(2)}, u32[]{:S(2)}) collective-permute-start(bf16[2,32,1536]{2,1,0:T(8,128)(2,1)S(1)} %add_convert_fusion.3), channel_id=1, source_target_pairs={{0,6},{1,3},{2,0},{3,5},{4,2},{5,7},{6,4},{7,1},{8,14},{9,11},{10,... | collective-permute-start | bytes 589832 | tf_op jit(solution)/shard_map/ppermute | solution.py:38
  128.3 4.2 %collective-permute-done.29 = bf16[2,32,1536]{2,1,0:T(8,128)(2,1)S(1)} collective-permute-done((bf16[2,32,1536]{2,1,0:T(8,128)(2,1)S(1)}, bf16[2,32,1536]{2,1,0:T(8,128)(2,1)S(1)}, u32[]{:S(2)}, u32[]{:S(2)}) %collective-permute-start.29) | collective-permute-done | bytes 196640 | tf_op jit(solution)/shard_map/ppermute | solution.py:38
  133.7 2.1 %collective-permute-done.26 = bf16[2,32,1536]{2,1,0:T(8,128)(2,1)S(1)} collective-permute-done((bf16[2,32,1536]{2,1,0:T(8,128)(2,1)S(1)}, bf16[2,32,1536]{2,1,0:T(8,128)(2,1)S(1)}, u32[]{:S(2)}, u32[]{:S(2)}) %collective-permute-start.26) | collective-permute-done | bytes 196640 | tf_op jit(solution)/shard_map/ppermute | solution.py:38
  137.3 3.9 %collective-permute-start.36 = (f32[2,1536]{1,0:T(2,128)S(1)}, f32[2,1536]{1,0:T(2,128)S(1)}, u32[]{:S(2)}, u32[]{:S(2)}) collective-permute-start(f32[2,1536]{1,0:T(2,128)S(1)} %fusion.1), channel_id=1, source_target_pairs={{0,4},{1,5},{2,6},{3,7},{4,0},{5,1},{6,2},{7,3},{8,12},{9,13},{10,... | collective-permute-start | bytes 36872 | tf_op jit(solution)/shard_map/ppermute | solution.py:38
  141.1 3.0 %mlp_weights.1 = (bf16[2,1536,384]{2,1,0:T(8,128)(2,1)}, bf16[384,1536]{1,0:T(8,128)(2,1)}) custom-call(bf16[4,32,1536]{2,1,0:T(8,128)(2,1)S(1)} %get-tuple-element.95.own_b.mids, bf16[4,32,1536]{2,1,0:T(8,128)(2,1)S(1)} %collective-permute-done.16.other, bf16[4,32,1536]{2,1,0:T(8,128)(2,1)S(1)} %collective-permute-done.17.near_0, ...), custom_call_target="tpu_custom_call" | custom-call | flops 905969664 | bytes 8073216 | tf_op jit(solution)/shard_map/mlp_weights/pallas_call | solution.py:82
  145.1 4.4 %collective-permute-start.31 = (bf16[32,1536]{1,0:T(8,128)(2,1)S(1)}, bf16[32,1536]{1,0:T(8,128)(2,1)S(1)}, u32[]{:S(2)}, u32[]{:S(2)}) collective-permute-start(bf16[32,1536]{1,0:T(8,128)(2,1)S(1)} %get-tuple-element.107), channel_id=1, source_target_pairs={{0,8},{8,16},{16,24},{24,32},{32,40},{40,48},{48,56},{56,64},{64,7... | collective-permute-start | bytes 294920 | tf_op jit(solution)/shard_map/ppermute | solution.py:344
  151.4 2.3 %collective-permute-done.31 = bf16[32,1536]{1,0:T(8,128)(2,1)S(1)} collective-permute-done((bf16[32,1536]{1,0:T(8,128)(2,1)S(1)}, bf16[32,1536]{1,0:T(8,128)(2,1)S(1)}, u32[]{:S(2)}, u32[]{:S(2)}) %collective-permute-start.31) | collective-permute-done | bytes 98336 | tf_op jit(solution)/shard_map/ppermute | solution.py:344
  153.7 2.6 %collective-permute-done.32 = bf16[32,1536]{1,0:T(8,128)(2,1)S(1)} collective-permute-done((bf16[32,1536]{1,0:T(8,128)(2,1)S(1)}, bf16[32,1536]{1,0:T(8,128)(2,1)S(1)}, u32[]{:S(2)}, u32[]{:S(2)}) %collective-permute-start.32) | collective-permute-done | bytes 98336 | tf_op jit(solution)/shard_map/ppermute | solution.py:344
  (84 shorter events, 32.2 us)
Async XLA Ops:
  2.4 7.5 %collective-permute-start.3 = (bf16[2,32,1536]{2,1,0:T(8,128)(2,1)S(1)}, bf16[2,32,1536]{2,1,0:T(8,128)(2,1)S(1)}, u32[]{:S(2)}, u32[]{:S(2)}) collective-permute-start(bf16[2,32,1536]{2,1,0:T(8,128)(2,1)S(1)} %constant_dynamic-update-slice_fusion.own_b), channel_id=1, source_target_pairs={{0,1},{1,0},{2,3},{3,2},{4,5},{5,4},{6,7},{7,6},{8,9},{9,8},{10,11... | collective-permute-start | bytes 589832 | tf_op jit(solution)/shard_map/ppermute | solution.py:38
  5.7 7.8 %collective-permute-start = (bf16[2,32,1536]{2,1,0:T(8,128)(2,1)S(1)}, bf16[2,32,1536]{2,1,0:T(8,128)(2,1)S(1)}, u32[]{:S(2)}, u32[]{:S(2)}) collective-permute-start(bf16[2,32,1536]{2,1,0:T(8,128)(2,1)S(1)} %constant_dynamic-update-slice_fusion.own_b), channel_id=1, source_target_pairs={{0,2},{1,7},{2,4},{3,1},{4,6},{5,3},{6,0},{7,5},{8,10},{9,15},{10,... | collective-permute-start | bytes 589832 | tf_op jit(solution)/shard_map/ppermute | solution.py:38
  10.0 7.7 %collective-permute-start.4 = (bf16[2,32,1536]{2,1,0:T(8,128)(2,1)S(1)}, bf16[2,32,1536]{2,1,0:T(8,128)(2,1)S(1)}, u32[]{:S(2)}, u32[]{:S(2)}) collective-permute-start(bf16[2,32,1536]{2,1,0:T(8,128)(2,1)S(1)} %collective-permute-done.3.other), channel_id=1, source_target_pairs={{0,2},{1,7},{2,4},{3,1},{4,6},{5,3},{6,0},{7,5},{8,10},{9,15},{10,... | collective-permute-start | bytes 589832 | tf_op jit(solution)/shard_map/ppermute | solution.py:38
  13.5 12.5 %collective-permute-start.1 = (bf16[2,32,1536]{2,1,0:T(8,128)(2,1)S(1)}, bf16[2,32,1536]{2,1,0:T(8,128)(2,1)S(1)}, u32[]{:S(2)}, u32[]{:S(2)}) collective-permute-start(bf16[2,32,1536]{2,1,0:T(8,128)(2,1)S(1)} %collective-permute-done.near_0), channel_id=1, source_target_pairs={{0,2},{1,7},{2,4},{3,1},{4,6},{5,3},{6,0},{7,5},{8,10},{9,15},{10,... | collective-permute-start | bytes 589832 | tf_op jit(solution)/shard_map/ppermute | solution.py:38
  17.7 8.3 %collective-permute-start.6 = (bf16[2,32,1536]{2,1,0:T(8,128)(2,1)S(1)}, bf16[2,32,1536]{2,1,0:T(8,128)(2,1)S(1)}, u32[]{:S(2)}, u32[]{:S(2)}) collective-permute-start(bf16[2,32,1536]{2,1,0:T(8,128)(2,1)S(1)} %collective-permute-done.4.near_1), channel_id=1, source_target_pairs={{0,1},{1,0},{2,3},{3,2},{4,5},{5,4},{6,7},{7,6},{8,9},{9,8},{10,11... | collective-permute-start | bytes 589832 | tf_op jit(solution)/shard_map/ppermute | solution.py:38
  19.8 16.3 %collective-permute-start.8 = (bf16[2,256,384]{2,1,0:T(8,128)(2,1)}, bf16[2,256,384]{2,1,0:T(8,128)(2,1)S(1)}, u32[]{:S(2)}, u32[]{:S(2)}) collective-permute-start(bf16[2,256,384]{2,1,0:T(8,128)(2,1)} %bitcast.47), channel_id=1, source_target_pairs={{0,248},{8,240},{16,232},{24,224},{32,216},{40,208},{48,200},{56,1... | collective-permute-start | bytes 1179656 | tf_op jit(solution)/shard_map/ppermute | solution.py:349
  25.7 10.2 %collective-permute-start.5 = (bf16[2,32,1536]{2,1,0:T(8,128)(2,1)S(1)}, bf16[2,32,1536]{2,1,0:T(8,128)(2,1)S(1)}, u32[]{:S(2)}, u32[]{:S(2)}) collective-permute-start(bf16[2,32,1536]{2,1,0:T(8,128)(2,1)S(1)} %collective-permute-done.near_0), channel_id=1, source_target_pairs={{0,1},{1,0},{2,3},{3,2},{4,5},{5,4},{6,7},{7,6},{8,9},{9,8},{10,11... | collective-permute-start | bytes 589832 | tf_op jit(solution)/shard_map/ppermute | solution.py:38
  26.0 10.0 %collective-permute-start.7 = (bf16[2,32,1536]{2,1,0:T(8,128)(2,1)S(1)}, bf16[2,32,1536]{2,1,0:T(8,128)(2,1)S(1)}, u32[]{:S(2)}, u32[]{:S(2)}) collective-permute-start(bf16[2,32,1536]{2,1,0:T(8,128)(2,1)S(1)} %collective-permute-done.1.far), channel_id=1, source_target_pairs={{0,1},{1,0},{2,3},{3,2},{4,5},{5,4},{6,7},{7,6},{8,9},{9,8},{10,11... | collective-permute-start | bytes 589832 | tf_op jit(solution)/shard_map/ppermute | solution.py:38
  28.2 18.4 %collective-permute-start.2 = (bf16[1920,128]{1,0:T(8,128)(2,1)S(1)}, bf16[1920,128]{1,0:T(8,128)(2,1)S(1)}, u32[]{:S(2)}, u32[]{:S(2)}) collective-permute-start(bf16[1920,128]{1,0:T(8,128)(2,1)S(1)} %pack_held.1), channel_id=1, source_target_pairs={{0,248},{8,240},{16,232},{24,224},{32,216},{40,208},{48,200},{56,1... | collective-permute-start | bytes 1474568 | tf_op jit(solution)/shard_map/ppermute | solution.py:349
  40.7 6.2 %collective-permute-start.13 = (bf16[2,32,1536]{2,1,0:T(8,128)(2,1)S(1)}, bf16[2,32,1536]{2,1,0:T(8,128)(2,1)S(1)}, u32[]{:S(2)}, u32[]{:S(2)}) collective-permute-start(bf16[2,32,1536]{2,1,0:T(8,128)(2,1)S(1)} %get-tuple-element.80), channel_id=1, source_target_pairs={{0,1},{1,0},{2,3},{3,2},{4,5},{5,4},{6,7},{7,6},{8,9},{9,8},{10,11... | collective-permute-start | bytes 589832 | tf_op jit(solution)/shard_map/ppermute | solution.py:38
  41.0 16.3 %collective-permute-start.9 = (bf16[2,32,1536]{2,1,0:T(8,128)(2,1)S(1)}, bf16[2,32,1536]{2,1,0:T(8,128)(2,1)S(1)}, u32[]{:S(2)}, u32[]{:S(2)}) collective-permute-start(bf16[2,32,1536]{2,1,0:T(8,128)(2,1)S(1)} %get-tuple-element.74), channel_id=1, source_target_pairs={{0,1},{1,0},{2,3},{3,2},{4,5},{5,4},{6,7},{7,6},{8,9},{9,8},{10,11... | collective-permute-start | bytes 589832 | tf_op jit(solution)/shard_map/ppermute | solution.py:38
  47.0 8.2 %collective-permute-start.14 = (bf16[2,32,1536]{2,1,0:T(8,128)(2,1)S(1)}, bf16[2,32,1536]{2,1,0:T(8,128)(2,1)S(1)}, u32[]{:S(2)}, u32[]{:S(2)}) collective-permute-start(bf16[2,32,1536]{2,1,0:T(8,128)(2,1)S(1)} %add_convert_fusion.6), channel_id=1, source_target_pairs={{0,6},{1,3},{2,0},{3,5},{4,2},{5,7},{6,4},{7,1},{8,14},{9,11},{10,... | collective-permute-start | bytes 589832 | tf_op jit(solution)/shard_map/ppermute | solution.py:38
  50.1 8.0 %collective-permute-start.11 = (bf16[2,32,1536]{2,1,0:T(8,128)(2,1)S(1)}, bf16[2,32,1536]{2,1,0:T(8,128)(2,1)S(1)}, u32[]{:S(2)}, u32[]{:S(2)}) collective-permute-start(bf16[2,32,1536]{2,1,0:T(8,128)(2,1)S(1)} %add_convert_fusion.8), channel_id=1, source_target_pairs={{0,6},{1,3},{2,0},{3,5},{4,2},{5,7},{6,4},{7,1},{8,14},{9,11},{10,... | collective-permute-start | bytes 589832 | tf_op jit(solution)/shard_map/ppermute | solution.py:38
  55.3 7.4 %collective-permute-start.15 = (bf16[2,32,1536]{2,1,0:T(8,128)(2,1)S(1)}, bf16[2,32,1536]{2,1,0:T(8,128)(2,1)S(1)}, u32[]{:S(2)}, u32[]{:S(2)}) collective-permute-start(bf16[2,32,1536]{2,1,0:T(8,128)(2,1)S(1)} %add_convert_fusion.5), channel_id=1, source_target_pairs={{0,1},{1,0},{2,3},{3,2},{4,5},{5,4},{6,7},{7,6},{8,9},{9,8},{10,11... | collective-permute-start | bytes 589832 | tf_op jit(solution)/shard_map/ppermute | solution.py:38
  58.2 9.3 %collective-permute-start.12 = (bf16[2,32,1536]{2,1,0:T(8,128)(2,1)S(1)}, bf16[2,32,1536]{2,1,0:T(8,128)(2,1)S(1)}, u32[]{:S(2)}, u32[]{:S(2)}) collective-permute-start(bf16[2,32,1536]{2,1,0:T(8,128)(2,1)S(1)} %add_convert_fusion.7), channel_id=1, source_target_pairs={{0,6},{1,3},{2,0},{3,5},{4,2},{5,7},{6,4},{7,1},{8,14},{9,11},{10,... | collective-permute-start | bytes 589832 | tf_op jit(solution)/shard_map/ppermute | solution.py:38
  68.3 7.8 %collective-permute-start.16 = (bf16[4,32,1536]{2,1,0:T(8,128)(2,1)S(1)}, bf16[4,32,1536]{2,1,0:T(8,128)(2,1)S(1)}, u32[]{:S(2)}, u32[]{:S(2)}) collective-permute-start(bf16[4,32,1536]{2,1,0:T(8,128)(2,1)S(1)} %get-tuple-element.95.own_b.mids), channel_id=1, source_target_pairs={{0,1},{1,0},{2,3},{3,2},{4,5},{5,4},{6,7},{7,6},{8,9},{9,8},{10,11... | collective-permute-start | bytes 1179656 | tf_op jit(solution)/shard_map/ppermute | solution.py:38
  71.9 11.5 %collective-permute-start.17 = (bf16[4,32,1536]{2,1,0:T(8,128)(2,1)S(1)}, bf16[4,32,1536]{2,1,0:T(8,128)(2,1)S(1)}, u32[]{:S(2)}, u32[]{:S(2)}) collective-permute-start(bf16[4,32,1536]{2,1,0:T(8,128)(2,1)S(1)} %get-tuple-element.95.own_b.mids), channel_id=1, source_target_pairs={{0,2},{1,7},{2,4},{3,1},{4,6},{5,3},{6,0},{7,5},{8,10},{9,15},{10,... | collective-permute-start | bytes 1179656 | tf_op jit(solution)/shard_map/ppermute | solution.py:38
  76.2 13.6 %collective-permute-start.18 = (bf16[4,32,1536]{2,1,0:T(8,128)(2,1)S(1)}, bf16[4,32,1536]{2,1,0:T(8,128)(2,1)S(1)}, u32[]{:S(2)}, u32[]{:S(2)}) collective-permute-start(bf16[4,32,1536]{2,1,0:T(8,128)(2,1)S(1)} %collective-permute-done.16.other), channel_id=1, source_target_pairs={{0,2},{1,7},{2,4},{3,1},{4,6},{5,3},{6,0},{7,5},{8,10},{9,15},{10,... | collective-permute-start | bytes 1179656 | tf_op jit(solution)/shard_map/ppermute | solution.py:38
  83.3 18.2 %collective-permute-start.19 = (bf16[4,32,1536]{2,1,0:T(8,128)(2,1)S(1)}, bf16[4,32,1536]{2,1,0:T(8,128)(2,1)S(1)}, u32[]{:S(2)}, u32[]{:S(2)}) collective-permute-start(bf16[4,32,1536]{2,1,0:T(8,128)(2,1)S(1)} %collective-permute-done.17.near_0), channel_id=1, source_target_pairs={{0,2},{1,7},{2,4},{3,1},{4,6},{5,3},{6,0},{7,5},{8,10},{9,15},{10,... | collective-permute-start | bytes 1179656 | tf_op jit(solution)/shard_map/ppermute | solution.py:38
  89.8 11.7 %collective-permute-start.21 = (bf16[4,32,1536]{2,1,0:T(8,128)(2,1)S(1)}, bf16[4,32,1536]{2,1,0:T(8,128)(2,1)S(1)}, u32[]{:S(2)}, u32[]{:S(2)}) collective-permute-start(bf16[4,32,1536]{2,1,0:T(8,128)(2,1)S(1)} %collective-permute-done.18.near_1), channel_id=1, source_target_pairs={{0,1},{1,0},{2,3},{3,2},{4,5},{5,4},{6,7},{7,6},{8,9},{9,8},{10,11... | collective-permute-start | bytes 1179656 | tf_op jit(solution)/shard_map/ppermute | solution.py:38
  103.0 17.2 %collective-permute-start.24 = (bf16[1920,128]{1,0:T(8,128)(2,1)S(1)}, bf16[1920,128]{1,0:T(8,128)(2,1)S(1)}, u32[]{:S(2)}, u32[]{:S(2)}) collective-permute-start(bf16[1920,128]{1,0:T(8,128)(2,1)S(1)} %pack_new.1), channel_id=1, source_target_pairs={{0,248},{8,240},{16,232},{24,224},{32,216},{40,208},{48,200},{56,1... | collective-permute-start | bytes 1474568 | tf_op jit(solution)/shard_map/ppermute | solution.py:349
  110.9 12.0 %collective-permute-start.34 = (f32[2,1536]{1,0:T(2,128)S(1)}, f32[2,1536]{1,0:T(2,128)S(1)}, u32[]{:S(2)}, u32[]{:S(2)}) collective-permute-start(f32[2,1536]{1,0:T(2,128)S(1)} %pad_maximum_fusion), channel_id=1, source_target_pairs={{0,1},{1,0},{2,3},{3,2},{4,5},{5,4},{6,7},{7,6},{8,9},{9,8},{10,11... | collective-permute-start | bytes 36872 | tf_op jit(solution)/shard_map/ppermute | solution.py:38
  121.6 12.1 %collective-permute-start.23 = (bf16[2,32,1536]{2,1,0:T(8,128)(2,1)S(1)}, bf16[2,32,1536]{2,1,0:T(8,128)(2,1)S(1)}, u32[]{:S(2)}, u32[]{:S(2)}) collective-permute-start(bf16[2,32,1536]{2,1,0:T(8,128)(2,1)S(1)} %get-tuple-element.98), channel_id=1, source_target_pairs={{0,1},{1,0},{2,3},{3,2},{4,5},{5,4},{6,7},{7,6},{8,9},{9,8},{10,11... | collective-permute-start | bytes 589832 | tf_op jit(solution)/shard_map/ppermute | solution.py:38
  122.9 14.3 %collective-permute-start.35 = (f32[2,1536]{1,0:T(2,128)S(1)}, f32[2,1536]{1,0:T(2,128)S(1)}, u32[]{:S(2)}, u32[]{:S(2)}) collective-permute-start(f32[2,1536]{1,0:T(2,128)S(1)} %fusion), channel_id=1, source_target_pairs={{0,2},{1,3},{2,0},{3,1},{4,6},{5,7},{6,4},{7,5},{8,10},{9,11},{10,... | collective-permute-start | bytes 36872 | tf_op jit(solution)/shard_map/ppermute | solution.py:38
  123.9 8.7 %collective-permute-start.29 = (bf16[2,32,1536]{2,1,0:T(8,128)(2,1)S(1)}, bf16[2,32,1536]{2,1,0:T(8,128)(2,1)S(1)}, u32[]{:S(2)}, u32[]{:S(2)}) collective-permute-start(bf16[2,32,1536]{2,1,0:T(8,128)(2,1)S(1)} %add_convert_fusion.1), channel_id=1, source_target_pairs={{0,6},{1,3},{2,0},{3,5},{4,2},{5,7},{6,4},{7,1},{8,14},{9,11},{10,... | collective-permute-start | bytes 589832 | tf_op jit(solution)/shard_map/ppermute | solution.py:38
  125.6 10.3 %collective-permute-start.26 = (bf16[2,32,1536]{2,1,0:T(8,128)(2,1)S(1)}, bf16[2,32,1536]{2,1,0:T(8,128)(2,1)S(1)}, u32[]{:S(2)}, u32[]{:S(2)}) collective-permute-start(bf16[2,32,1536]{2,1,0:T(8,128)(2,1)S(1)} %add_convert_fusion.3), channel_id=1, source_target_pairs={{0,6},{1,3},{2,0},{3,5},{4,2},{5,7},{6,4},{7,1},{8,14},{9,11},{10,... | collective-permute-start | bytes 589832 | tf_op jit(solution)/shard_map/ppermute | solution.py:38
  132.6 11.7 %collective-permute-start.30 = (bf16[2,32,1536]{2,1,0:T(8,128)(2,1)S(1)}, bf16[2,32,1536]{2,1,0:T(8,128)(2,1)S(1)}, u32[]{:S(2)}, u32[]{:S(2)}) collective-permute-start(bf16[2,32,1536]{2,1,0:T(8,128)(2,1)S(1)} %add_convert_fusion), channel_id=1, source_target_pairs={{0,1},{1,0},{2,3},{3,2},{4,5},{5,4},{6,7},{7,6},{8,9},{9,8},{10,11... | collective-permute-start | bytes 589832 | tf_op jit(solution)/shard_map/ppermute | solution.py:38
  135.9 8.9 %collective-permute-start.27 = (bf16[2,32,1536]{2,1,0:T(8,128)(2,1)S(1)}, bf16[2,32,1536]{2,1,0:T(8,128)(2,1)S(1)}, u32[]{:S(2)}, u32[]{:S(2)}) collective-permute-start(bf16[2,32,1536]{2,1,0:T(8,128)(2,1)S(1)} %add_convert_fusion.2), channel_id=1, source_target_pairs={{0,6},{1,3},{2,0},{3,5},{4,2},{5,7},{6,4},{7,1},{8,14},{9,11},{10,... | collective-permute-start | bytes 589832 | tf_op jit(solution)/shard_map/ppermute | solution.py:38
  137.3 13.5 %collective-permute-start.36 = (f32[2,1536]{1,0:T(2,128)S(1)}, f32[2,1536]{1,0:T(2,128)S(1)}, u32[]{:S(2)}, u32[]{:S(2)}) collective-permute-start(f32[2,1536]{1,0:T(2,128)S(1)} %fusion.1), channel_id=1, source_target_pairs={{0,4},{1,5},{2,6},{3,7},{4,0},{5,1},{6,2},{7,3},{8,12},{9,13},{10,... | collective-permute-start | bytes 36872 | tf_op jit(solution)/shard_map/ppermute | solution.py:38
  144.2 13.3 %collective-permute-start.33 = (bf16[2,256,384]{2,1,0:T(8,128)(2,1)S(1)}, bf16[2,256,384]{2,1,0:T(8,128)(2,1)S(1)}, u32[]{:S(2)}, u32[]{:S(2)}) collective-permute-start(bf16[2,256,384]{2,1,0:T(8,128)(2,1)S(1)} %get-tuple-element.111.kept), channel_id=1, source_target_pairs={{0,248},{8,240},{16,232},{24,224},{32,216},{40,208},{48,200},{56,1... | collective-permute-start | bytes 1179656 | tf_op jit(solution)/shard_map/ppermute | solution.py:349
  145.1 8.6 %collective-permute-start.31 = (bf16[32,1536]{1,0:T(8,128)(2,1)S(1)}, bf16[32,1536]{1,0:T(8,128)(2,1)S(1)}, u32[]{:S(2)}, u32[]{:S(2)}) collective-permute-start(bf16[32,1536]{1,0:T(8,128)(2,1)S(1)} %get-tuple-element.107), channel_id=1, source_target_pairs={{0,8},{8,16},{16,24},{24,32},{32,40},{40,48},{48,56},{56,64},{64,7... | collective-permute-start | bytes 294920 | tf_op jit(solution)/shard_map/ppermute | solution.py:344
  149.5 6.8 %collective-permute-start.32 = (bf16[32,1536]{1,0:T(8,128)(2,1)S(1)}, bf16[32,1536]{1,0:T(8,128)(2,1)S(1)}, u32[]{:S(2)}, u32[]{:S(2)}) collective-permute-start(bf16[32,1536]{1,0:T(8,128)(2,1)S(1)} %get-tuple-element.108), channel_id=1, source_target_pairs={{8,0},{16,8},{24,16},{32,24},{40,32},{48,40},{56,48},{64,56},{72,6... | collective-permute-start | bytes 294920 | tf_op jit(solution)/shard_map/ppermute | solution.py:344
  (12 other events, 123.5 us)
where the time goes:
time: 162 us; the launch traced here: 160 us
  starting transfers between devices  80.9 us (50%)
  waiting for transfers between devices  49.9 us (31%)
  Pallas kernels  22.4 us (14%)
  local copies, waits for them, and re-layouts  4.99 us (3%)
    ppermute x31, starting transfers between devices, over(): return lax.ppermute(value, 'tensor', pairs)  64.3 us
    ppermute x31, waiting for transfers between devices, over(): return lax.ppermute(value, 'tensor', pairs)  29.4 us
    pallas_call x12, Pallas kernels, call(): pl.pallas_call(body, name=name, out_shape=outs, in_specs=[hbm if i in str...  22.4 us
    ppermute x4, waiting for transfers between devices, mirrored(): lax.ppermute(value, 'section', [(i, count - 1 - i) for i in range(count)])  15.7 us
    ppermute x4, starting transfers between devices, mirrored(): lax.ppermute(value, 'section', [(i, count - 1 - i) for i in range(count)])  11 us
    ppermute x2, starting transfers between devices, shifted(): return lax.ppermute(value, 'section', pairs)  5.68 us
    ppermute x2, waiting for transfers between devices, shifted(): return lax.ppermute(value, 'section', pairs)  4.85 us
    unnamed x17, local copies, waits for them, and re-layouts  4.09 us
  transfers between devices with their start and end apart: 37, of which 18 were waited for; matrix products, arithmetic and copies ran while one was open for 1% of the time, Pallas kernels for 13%

commit v1 on v0

--- a/solution.py
+++ b/solution.py
@@ -46,28 +46,30 @@
     return (one.astype(F32) + other.astype(F32)).astype(BF)
 
 
-def gather(own):
+def gather(own, before_far=(), before_s0=lambda near_0: ()):
     near_0, other = over(own, GATHER), over(own, CORE)
-    near_1, far = over(other, GATHER), over(near_0, GATHER)
+    near_1, far = over(other, GATHER), over(after(near_0, *before_far), GATHER)
     s_1 = over(near_1, CORE)
-    return own, other, near_0, near_1, far, over(near_0, CORE), s_1, over(after(far, s_1), CORE)
-
-
-def reduce_blocks(parts):
+    return own, other, near_0, near_1, far, over(after(near_0, *before_s0(near_0)), CORE), s_1, over(after(far, s_1), CORE)
+
+
+def start_sums(parts, *before_near):
     held_2 = add(parts[4], over(parts[7], CORE))
     far = over(held_2, REDUCE)
-    held_1 = add(parts[3], over(parts[6], CORE))
-    near_1 = over(held_1, REDUCE)
-    held_0 = add(add(parts[2], over(parts[5], CORE)), far)
-    near_0 = over(held_0, REDUCE)
-    other = add(parts[1], near_1)
-    return (parts[0], near_0, over(other, CORE)), other
-
-
-def all_sum(value):
-    for pairs in (CORE, [(t, t ^ 2) for t in range(8)], [(t, t ^ 4) for t in range(8)]):
-        value = value + over(value, pairs)
-    return value
+    held_1 = add(parts[3], over(after(parts[6], held_2, *before_near), CORE))
+    return held_2, held_1, far, add(parts[1], over(held_1, REDUCE))
+
+
+def last_held(parts, far):
+    return add(add(parts[2], over(parts[5], CORE)), far)
+
+
+def end_sums(parts, held_0, other):
+    return parts[0], over(held_0, REDUCE), over(other, CORE)
+
+
+def add_across(value, bit):
+    return value + over(value, [(t, t ^ bit) for t in range(8)])
 
 
 def call(body, name, outs, scratch, flops, args, streamed=()):
@@ -77,8 +79,8 @@
         pltpu.with_memory_space_constraint(a, pltpu.HBM) if i in streamed else a
         for i, a in enumerate(args)
     ]
-    moved = sum(a.size * a.dtype.itemsize for a in args)
-    moved += sum(math.prod(o.shape) * o.dtype.itemsize for o in outs)
+    moved = 0 if flops < 4096 else sum(a.size * a.dtype.itemsize for a in args)
+    moved += 1024 if flops < 4096 else sum(math.prod(o.shape) * o.dtype.itemsize for o in outs)
     return pl.pallas_call(
         body,
         name=name,
@@ -193,16 +195,21 @@
     return powers / jnp.sum(powers, axis=0, keepdims=True)
 
 
-def bring(*refs):
-    count = len(refs) // 3
-    copies = [
-        pltpu.make_async_copy(*each)
-        for each in zip(refs[:count], refs[count : 2 * count], refs[2 * count :])
-    ]
+def copy_all(copies):
+    copies = [pltpu.make_async_copy(*each) for each in copies]
     for copy in copies:
         copy.start()
     for copy in copies:
         copy.wait()
+
+
+def bring(*refs):
+    count = len(refs) // 3
+    copy_all(zip(refs[:count], refs[count : 2 * count], refs[2 * count :]))
+
+
+def stack(one, other, out, first, second):
+    copy_all(((one, out.at[0], first), (other, out.at[1], second)))
 
 
 def forward_attention(gains, wqkv, wout, qkv, full, mixed, total):
@@ -362,15 +369,18 @@
     full, total = pltpu.VMEM((256, D), BF), pltpu.VMEM((256, D), F32)
     per_head, pair = pltpu.VMEM((192, 256), BF), pltpu.VMEM((2, 32, D), BF)
 
-    blocks = gather(jnp.stack([layer_in, dy]))
-    fetched_g = mirrored(after(held_g, blocks[3]))
-    (packed,) = call(pack_held, "pack_held", [shape(STASH, 128)], [], 1024, (held_x, held_q))
-    fetched = mirrored(after(packed, blocks[4]))
-    weights = [after(wqkv, blocks[1]), wout, held_g, wdown, wgateup]
+    own = call(
+        stack, "stack", [shape(2, 32, D)], [pltpu.SemaphoreType.DMA(())] * 2, 8192, (layer_in, dy), (0, 1)
+    )[0]
+    fetched_g = mirrored(after(held_g, own))
+    weights = [after(wqkv, own), wout, held_g, wdown, wgateup]
     wqkv, wout, held_g, wdown, wgateup = call(
         bring, "bring", [pltpu.VMEM(w.shape, w.dtype) for w in weights],
-        [pltpu.SemaphoreType.DMA(()) for _ in weights], 0, weights, (0, 1, 2, 3, 4),
-    )
+        [pltpu.SemaphoreType.DMA(()) for _ in weights], 8192, weights, (0, 1, 2, 3, 4),
+    )
+    (packed,) = call(pack_held, "pack_held", [shape(STASH, 128)], [], 8192, (held_x, after(held_q, own)))
+    blocks = gather(own, (wqkv, packed), lambda _: (fetched_g,))
+    fetched = mirrored(after(packed, blocks[4]))
 
     qkv, dgateup, act_low, grads, *parts = call(
         first_stage, "first_stage",
@@ -380,7 +390,8 @@
         (swapped_pairs, *blocks, gains, fetched_g, wqkv, wout, held_g, wdown, wgateup),
     )
     parts[7] = after(parts[7], fetched)
-    sums, _ = reduce_blocks(parts)
+    _, _, far, other = start_sums(parts)
+    sums = end_sums(parts, last_held(parts, far), other)
     mids, mid_terms = call(
         middle, "middle", [shape(4, 32, D), shape(1, D, dtype=F32)], [pair],
         32 * D * 40, (swapped_pairs, held_x, fetched, layer_in, dy, *sums, gains),
@@ -389,9 +400,9 @@
     stash_q, mixed, probs = call(
         backward_probs, "backward_probs",
         [shape(3, 192, 256), shape(192, 256), shape(2, 256, 256, dtype=F32)], [],
-        mega * 128, (swapped_pairs, held_q, fetched),
-    )
-    blocks = gather(mids)
+        1024, (swapped_pairs, held_q, fetched),
+    )
+    blocks = gather(mids, (probs,))
     (packed,) = call(pack_new, "pack_new", [shape(STASH, 128)], [pair], 1024, (layer_in, mids, qkv))
     moved = mirrored(after(packed, blocks[2]))
 
@@ -399,39 +410,43 @@
         second_stage, "second_stage",
         [shape(2, 256, 384), shape(3, 192, 256), shape(256, D)] + SPREAD,
         [full, per_head, total],
-        mega * 2150,
+        1024,
         (*blocks, gains, stash_q, probs, wgateup, wdown, wout, wqkv),
     )
-    parts[7] = after(parts[7], moved)
-    sums, other = reduce_blocks(parts)
-    moved_gateup = mirrored(after(gateup, other))
 
     grad_qkv, grad_out, in_terms = call(
         attention_weights, "attention_weights",
         [shape(3, 192, D), shape(192, D), shape(1, D, dtype=F32)], [full],
-        mega * 768, (*blocks, gains, dqkv, mixed, dmid, wqkv),
+        1024, (*blocks, gains, dqkv, mixed, dmid, wqkv),
     )
     grad_gateup, grad_down = call(
         mlp_weights, "mlp_weights",
         [shape(2, D, 384), shape(384, D)], [full],
-        mega * 1152, (*blocks, gains, dgateup, act_low, after(grads, gateup)),
-    )
+        1024, (*blocks, gains, dgateup, act_low, after(grads, gateup)),
+    )
+    parts[7] = after(parts[7], moved, in_terms, grad_down)
+    held_2, held_1, far, other = start_sums(parts)
+    moved_gateup = mirrored(after(gateup, other))
+    terms = add_across(jnp.concatenate([in_terms, mid_terms]), 1)
+    terms = add_across(after(terms, held_2), 2)
+    stash_inputs, stash_qkv = call(
+        stash_out, "stash_out", [shape(*part) for part in PARTS], [pair],
+        1024, (swapped_pairs, after(moved, held_2), layer_in, mids, qkv),
+    )
+    held_0 = after(last_held(parts, far), terms, stash_inputs)
+    grad_gains = add_across(after(terms, held_0), 4)
+    sums = end_sums(parts, held_0, other)
     layer_out, dinput = call(
         last, "last", [shape(32, D), shape(32, D)], [],
-        32 * D * 40, (after(mids, grad_down, in_terms), *sums, gains),
+        32 * D * 40, (mids, *sums, gains),
     )
     forward_sent = shifted(layer_out, 1)
     backward_sent = shifted(dinput, -1)
-    grad_gains = all_sum(jnp.concatenate([in_terms, mid_terms]))
-
-    stash_inputs, stash_qkv = call(
-        stash_out, "stash_out", [shape(*part) for part in PARTS], [pair],
-        1024, (swapped_pairs, moved, layer_in, mids, qkv),
-    )
     (stash_gateup,) = call(
         stash_out_last, "stash_out_last", [shape(2, 256, 384)], [],
         1024, (swapped_pairs, moved_gateup, gateup),
     )
+
     return (
         forward_sent[None],
         backward_sent[None],

time: 162 us -> 156 us (0.963)
  starting transfers between devices: 80.9 us -> 69.6 us
  waiting for transfers between devices: 49.9 us -> 57.3 us
  local copies, waits for them, and re-layouts: 4.99 us -> 3.21 us
    ppermute x31, waiting for transfers between devices: 29.4 us -> 42.4 us  [over(): return lax.ppermute(value, 'tensor', pairs)]
    ppermute x31, starting transfers between devices: 64.3 us -> 51.6 us  [over(): return lax.ppermute(value, 'tensor', pairs)]
    ppermute x4, waiting for transfers between devices: 15.7 us -> 5.91 us  [mirrored(): lax.ppermute(value, 'section', [(i, count - 1 - i) for i in range(count)])]
    ppermute x2, waiting for transfers between devices: 4.85 us -> 9 us  [shifted(): return lax.ppermute(value, 'section', pairs)]
    ppermute x2, starting transfers between devices: 5.68 us -> 8.4 us  [shifted(): return lax.ppermute(value, 'section', pairs)]
    pallas_call x12 -> x13, Pallas kernels: 22.4 us -> 23.3 us  [call(): pl.pallas_call(body, name=name, out_shape=outs, in_specs=[hbm if i in str...]
    unnamed x17 -> x18, local copies, waits for them, and re-layouts: 4.09 us -> 3.21 us
where the time goes in v1:
time: 156 us; the launch traced here: 155 us
  starting transfers between devices  69.6 us (45%)
  waiting for transfers between devices  57.3 us (37%)
  Pallas kernels  23.3 us (15%)
  local copies, waits for them, and re-layouts  3.21 us (2%)
    ppermute x31, starting transfers between devices, over(): return lax.ppermute(value, 'tensor', pairs)  51.6 us
    ppermute x31, waiting for transfers between devices, over(): return lax.ppermute(value, 'tensor', pairs)  42.4 us
    pallas_call x13, Pallas kernels, call(): pl.pallas_call(body, name=name, out_shape=outs, in_specs=[hbm if i in str...  23.3 us
    ppermute x4, starting transfers between devices, mirrored(): lax.ppermute(value, 'section', [(i, count - 1 - i) for i in range(count)])  9.64 us
    ppermute x2, waiting for transfers between devices, shifted(): return lax.ppermute(value, 'section', pairs)  9 us
    ppermute x2, starting transfers between devices, shifted(): return lax.ppermute(value, 'section', pairs)  8.4 us
    ppermute x4, waiting for transfers between devices, mirrored(): lax.ppermute(value, 'section', [(i, count - 1 - i) for i in range(count)])  5.91 us
    unnamed x18, local copies, waits for them, and re-layouts  3.21 us
  transfers between devices with their start and end apart: 37, of which 18 were waited for; matrix products, arithmetic and copies ran while one was open for 1% of the time, Pallas kernels for 13%

profile of v1, /device:TPU:1, one launch (start us, length us, event | category | flops | bytes accessed | tf_op | source)
XLA Modules:
  0.0 155.5 jit_solution(11503160084106277527)
XLA Ops:
  1.6 3.3 %collective-permute-start.3 = (bf16[2,32,1536]{2,1,0:T(8,128)(2,1)S(1)}, bf16[2,32,1536]{2,1,0:T(8,128)(2,1)S(1)}, u32[]{:S(2)}, u32[]{:S(2)}) collective-permute-start(bf16[2,32,1536]{2,1,0:T(8,128)(2,1)S(1)} %stack.1.own_b), channel_id=1, source_target_pairs={{0,1},{1,0},{2,3},{3,2},{4,5},{5,4},{6,7},{7,6},{8,9},{9,8},{10,11... | collective-permute-start | bytes 589832 | tf_op jit(solution)/shard_map/ppermute | solution.py:38
  4.9 4.3 %collective-permute-start = (bf16[2,32,1536]{2,1,0:T(8,128)(2,1)S(1)}, bf16[2,32,1536]{2,1,0:T(8,128)(2,1)S(1)}, u32[]{:S(2)}, u32[]{:S(2)}) collective-permute-start(bf16[2,32,1536]{2,1,0:T(8,128)(2,1)S(1)} %stack.1.own_b), channel_id=1, source_target_pairs={{0,2},{1,7},{2,4},{3,1},{4,6},{5,3},{6,0},{7,5},{8,10},{9,15},{10,... | collective-permute-start | bytes 589832 | tf_op jit(solution)/shard_map/ppermute | solution.py:38
  9.2 5.4 %collective-permute-start.5 = (bf16[2,256,384]{2,1,0:T(8,128)(2,1)}, bf16[2,256,384]{2,1,0:T(8,128)(2,1)S(1)}, u32[]{:S(2)}, u32[]{:S(2)}) collective-permute-start(bf16[2,256,384]{2,1,0:T(8,128)(2,1)} %bitcast.49), channel_id=1, source_target_pairs={{0,248},{8,240},{16,232},{24,224},{32,216},{40,208},{48,200},{56,1... | collective-permute-start | bytes 1179656 | tf_op jit(solution)/shard_map/ppermute | solution.py:356
  17.8 2.9 %bring.1 = (bf16[3,192,1536]{2,1,0:T(8,128)(2,1)S(1)}, bf16[192,1536]{1,0:T(8,128)(2,1)S(1)}, bf16[2,256,384]{2,1,0:T(8,128)(2,1)S(1)}, bf16[384,1536]{1,0:T(8,128)(2,1)S(1)}, bf16[2,1536,384]{2,1,0:T(8,128)(2,1)S(1)}) custom-call(bf16[3,192,1536]{2,1,0:T(8,128)(2,1)} %bitcast.46, bf16[192,1536]{1,0:T(8,128)(2,1)} %bitcast.48, ...), custom_call_target="tpu_custom_call" | custom-call | flops 8192 | bytes 12582912 | tf_op jit(solution)/shard_map/bring/pallas_call | solution.py:84
  21.1 10.8 %collective-permute-start.7 = (bf16[2,32,1536]{2,1,0:T(8,128)(2,1)S(1)}, bf16[2,32,1536]{2,1,0:T(8,128)(2,1)S(1)}, u32[]{:S(2)}, u32[]{:S(2)}) collective-permute-start(bf16[2,32,1536]{2,1,0:T(8,128)(2,1)S(1)} %collective-permute-done.4.near_1), channel_id=1, source_target_pairs={{0,1},{1,0},{2,3},{3,2},{4,5},{5,4},{6,7},{7,6},{8,9},{9,8},{10,11... | collective-permute-start | bytes 589832 | tf_op jit(solution)/shard_map/ppermute | solution.py:38
  31.9 2.7 %collective-permute-start.2 = (bf16[1920,128]{1,0:T(8,128)(2,1)S(1)}, bf16[1920,128]{1,0:T(8,128)(2,1)S(1)}, u32[]{:S(2)}, u32[]{:S(2)}) collective-permute-start(bf16[1920,128]{1,0:T(8,128)(2,1)S(1)} %pack_held.1), channel_id=1, source_target_pairs={{0,248},{8,240},{16,232},{24,224},{32,216},{40,208},{48,200},{56,1... | collective-permute-start | bytes 1474568 | tf_op jit(solution)/shard_map/ppermute | solution.py:356
  36.3 4.6 %first_stage.1 = (bf16[3,192,256]{2,1,0:T(8,128)(2,1)S(1)}, bf16[2,256,384]{2,1,0:T(8,128)(2,1)S(1)}, bf16[256,384]{1,0:T(8,128)(2,1)S(1)}, bf16[256,1536]{1,0:T...) custom-call(s32[16]{0:T(128)S(1)} %copy-done.7, ...), custom_call_target="tpu_custom_call" | custom-call | flops 1612185600 | bytes 11513920 | tf_op jit(solution)/shard_map/first_stage/pallas_call | solution.py:84
  40.9 5.8 %collective-permute-done.2.fetched = bf16[1920,128]{1,0:T(8,128)(2,1)S(1)} collective-permute-done((bf16[1920,128]{1,0:T(8,128)(2,1)S(1)}, bf16[1920,128]{1,0:T(8,128)(2,1)S(1)}, u32[]{:S(2)}, u32[]{:S(2)}) %collective-permute-start.2) | collective-permute-done | bytes 491552 | tf_op jit(solution)/shard_map/ppermute | solution.py:356
  46.7 3.0 %collective-permute-start.10 = (bf16[2,32,1536]{2,1,0:T(8,128)(2,1)S(1)}, bf16[2,32,1536]{2,1,0:T(8,128)(2,1)S(1)}, u32[]{:S(2)}, u32[]{:S(2)}) collective-permute-start(bf16[2,32,1536]{2,1,0:T(8,128)(2,1)S(1)} %get-tuple-element.89), channel_id=1, source_target_pairs={{0,1},{1,0},{2,3},{3,2},{4,5},{5,4},{6,7},{7,6},{8,9},{9,8},{10,11... | collective-permute-start | bytes 589832 | tf_op jit(solution)/shard_map/ppermute | solution.py:38
  52.4 2.3 %collective-permute-start.14 = (bf16[2,32,1536]{2,1,0:T(8,128)(2,1)S(1)}, bf16[2,32,1536]{2,1,0:T(8,128)(2,1)S(1)}, u32[]{:S(2)}, u32[]{:S(2)}) collective-permute-start(bf16[2,32,1536]{2,1,0:T(8,128)(2,1)S(1)} %add_convert_fusion.6), channel_id=1, source_target_pairs={{0,6},{1,3},{2,0},{3,5},{4,2},{5,7},{6,4},{7,1},{8,14},{9,11},{10,... | collective-permute-start | bytes 589832 | tf_op jit(solution)/shard_map/ppermute | solution.py:38
  54.8 4.6 %collective-permute-done.11 = bf16[2,32,1536]{2,1,0:T(8,128)(2,1)S(1)} collective-permute-done((bf16[2,32,1536]{2,1,0:T(8,128)(2,1)S(1)}, bf16[2,32,1536]{2,1,0:T(8,128)(2,1)S(1)}, u32[]{:S(2)}, u32[]{:S(2)}) %collective-permute-start.11) | collective-permute-done | bytes 196640 | tf_op jit(solution)/shard_map/ppermute | solution.py:38
  59.8 4.8 %collective-permute-done.14 = bf16[2,32,1536]{2,1,0:T(8,128)(2,1)S(1)} collective-permute-done((bf16[2,32,1536]{2,1,0:T(8,128)(2,1)S(1)}, bf16[2,32,1536]{2,1,0:T(8,128)(2,1)S(1)}, u32[]{:S(2)}, u32[]{:S(2)}) %collective-permute-start.14) | collective-permute-done | bytes 196640 | tf_op jit(solution)/shard_map/ppermute | solution.py:38
  64.8 3.8 %collective-permute-done.12.near = bf16[2,32,1536]{2,1,0:T(8,128)(2,1)S(1)} collective-permute-done((bf16[2,32,1536]{2,1,0:T(8,128)(2,1)S(1)}, bf16[2,32,1536]{2,1,0:T(8,128)(2,1)S(1)}, u32[]{:S(2)}, u32[]{:S(2)}) %collective-permute-start.12) | collective-permute-done | bytes 196640 | tf_op jit(solution)/shard_map/ppermute | solution.py:38
  70.9 2.6 %collective-permute-start.17 = (bf16[4,32,1536]{2,1,0:T(8,128)(2,1)S(1)}, bf16[4,32,1536]{2,1,0:T(8,128)(2,1)S(1)}, u32[]{:S(2)}, u32[]{:S(2)}) collective-permute-start(bf16[4,32,1536]{2,1,0:T(8,128)(2,1)S(1)} %get-tuple-element.94.own_b.mids), channel_id=1, source_target_pairs={{0,2},{1,7},{2,4},{3,1},{4,6},{5,3},{6,0},{7,5},{8,10},{9,15},{10,... | collective-permute-start | bytes 1179656 | tf_op jit(solution)/shard_map/ppermute | solution.py:38
  76.3 13.8 %collective-permute-done.17.near_0 = bf16[4,32,1536]{2,1,0:T(8,128)(2,1)S(1)} collective-permute-done((bf16[4,32,1536]{2,1,0:T(8,128)(2,1)S(1)}, bf16[4,32,1536]{2,1,0:T(8,128)(2,1)S(1)}, u32[]{:S(2)}, u32[]{:S(2)}) %collective-permute-start.17) | collective-permute-done | bytes 393248 | tf_op jit(solution)/shard_map/ppermute | solution.py:38
  90.1 2.8 %collective-permute-start.19 = (bf16[4,32,1536]{2,1,0:T(8,128)(2,1)S(1)}, bf16[4,32,1536]{2,1,0:T(8,128)(2,1)S(1)}, u32[]{:S(2)}, u32[]{:S(2)}) collective-permute-start(bf16[4,32,1536]{2,1,0:T(8,128)(2,1)S(1)} %collective-permute-done.17.near_0), channel_id=1, source_target_pairs={{0,2},{1,7},{2,4},{3,1},{4,6},{5,3},{6,0},{7,5},{8,10},{9,15},{10,... | collective-permute-start | bytes 1179656 | tf_op jit(solution)/shard_map/ppermute | solution.py:38
  92.8 1.4 collective-permute-done.18.near_1
  94.3 1.6 %collective-permute-start.21 = (bf16[4,32,1536]{2,1,0:T(8,128)(2,1)S(1)}, bf16[4,32,1536]{2,1,0:T(8,128)(2,1)S(1)}, u32[]{:S(2)}, u32[]{:S(2)}) collective-permute-start(bf16[4,32,1536]{2,1,0:T(8,128)(2,1)S(1)} %collective-permute-done.18.near_1), channel_id=1, source_target_pairs={{0,1},{1,0},{2,3},{3,2},{4,5},{5,4},{6,7},{7,6},{8,9},{9,8},{10,11... | collective-permute-start | bytes 1179656 | tf_op jit(solution)/shard_map/ppermute | solution.py:38
  96.2 2.3 %collective-permute-done.19.far = bf16[4,32,1536]{2,1,0:T(8,128)(2,1)S(1)} collective-permute-done((bf16[4,32,1536]{2,1,0:T(8,128)(2,1)S(1)}, bf16[4,32,1536]{2,1,0:T(8,128)(2,1)S(1)}, u32[]{:S(2)}, u32[]{:S(2)}) %collective-permute-start.19) | collective-permute-done | bytes 393248 | tf_op jit(solution)/shard_map/ppermute | solution.py:38
  98.5 3.8 %collective-permute-start.22 = (bf16[4,32,1536]{2,1,0:T(8,128)(2,1)S(1)}, bf16[4,32,1536]{2,1,0:T(8,128)(2,1)S(1)}, u32[]{:S(2)}, u32[]{:S(2)}) collective-permute-start(bf16[4,32,1536]{2,1,0:T(8,128)(2,1)S(1)} %collective-permute-done.19.far), channel_id=1, source_target_pairs={{0,1},{1,0},{2,3},{3,2},{4,5},{5,4},{6,7},{7,6},{8,9},{9,8},{10,11... | collective-permute-start | bytes 1179656 | tf_op jit(solution)/shard_map/ppermute | solution.py:38
  103.6 4.1 %second_stage.1 = (bf16[2,256,384]{2,1,0:T(8,128)(2,1)S(1)}, bf16[3,192,256]{2,1,0:T(8,128)(2,1)S(1)}, bf16[256,1536]{1,0:T(8,128)(2,1)S(1)}, bf16[2,32,1536]{2,...) custom-call(bf16[4,32,1536]{2,1,0:T(8,128)(2,1)S(1)} %get-tuple-elem, ...), custom_call_target="tpu_custom_call" | custom-call | flops 1024 | bytes 1024 | tf_op jit(solution)/shard_map/second_stage/pallas_call | solution.py:84
  107.7 2.3 %attention_weights.1 = (bf16[3,192,1536]{2,1,0:T(8,128)(2,1)}, bf16[192,1536]{1,0:T(8,128)(2,1)}, f32[1,1536]{1,0:T(1,128)S(1)}) custom-call(bf16[4,32,1536]{2,1,0:T(8,128)(2,1)S(1)} %get-tuple-element.94.own_b.mids, bf16[4,32,1536]{2,1,0:T(8,128)(2,1)S(1)} %collective-permute-done.16.other, bf16[4,32,1536]{2,1,0:T(8,128)(2,1)S(1)} %collective-permute-done.17.near_0, ...), custom_call_target="tpu_custom_call" | custom-call | flops 1024 | bytes 1024 | tf_op jit(solution)/shard_map/attention_weights/pallas_call | solution.py:84
  110.0 3.0 %mlp_weights.1 = (bf16[2,1536,384]{2,1,0:T(8,128)(2,1)}, bf16[384,1536]{1,0:T(8,128)(2,1)}) custom-call(bf16[4,32,1536]{2,1,0:T(8,128)(2,1)S(1)} %get-tuple-element.94.own_b.mids, bf16[4,32,1536]{2,1,0:T(8,128)(2,1)S(1)} %collective-permute-done.16.other, bf16[4,32,1536]{2,1,0:T(8,128)(2,1)S(1)} %collective-permute-done.17.near_0, ...), custom_call_target="tpu_custom_call" | custom-call | flops 1024 | bytes 1024 | tf_op jit(solution)/shard_map/mlp_weights/pallas_call | solution.py:84
  115.5 1.6 %collective-permute-start.28 = (f32[2,1536]{1,0:T(2,128)S(1)}, f32[2,1536]{1,0:T(2,128)S(1)}, u32[]{:S(2)}, u32[]{:S(2)}) collective-permute-start(f32[2,1536]{1,0:T(2,128)S(1)} %fusion), channel_id=1, source_target_pairs={{0,2},{1,3},{2,0},{3,1},{4,6},{5,7},{6,4},{7,5},{8,10},{9,11},{10,... | collective-permute-start | bytes 36872 | tf_op jit(solution)/shard_map/ppermute | solution.py:38
  118.4 1.5 stash_out.1
  120.0 2.4 %collective-permute-start.31 = (bf16[2,32,1536]{2,1,0:T(8,128)(2,1)S(1)}, bf16[2,32,1536]{2,1,0:T(8,128)(2,1)S(1)}, u32[]{:S(2)}, u32[]{:S(2)}) collective-permute-start(bf16[2,32,1536]{2,1,0:T(8,128)(2,1)S(1)} %add_convert_fusion.1), channel_id=1, source_target_pairs={{0,6},{1,3},{2,0},{3,5},{4,2},{5,7},{6,4},{7,1},{8,14},{9,11},{10,... | collective-permute-start | bytes 589832 | tf_op jit(solution)/shard_map/ppermute | solution.py:38
  122.3 3.5 %collective-permute-done.26 = bf16[2,32,1536]{2,1,0:T(8,128)(2,1)S(1)} collective-permute-done((bf16[2,32,1536]{2,1,0:T(8,128)(2,1)S(1)}, bf16[2,32,1536]{2,1,0:T(8,128)(2,1)S(1)}, u32[]{:S(2)}, u32[]{:S(2)}) %collective-permute-start.26) | collective-permute-done | bytes 196640 | tf_op jit(solution)/shard_map/ppermute | solution.py:38
  127.0 3.2 %collective-permute-done.31 = bf16[2,32,1536]{2,1,0:T(8,128)(2,1)S(1)} collective-permute-done((bf16[2,32,1536]{2,1,0:T(8,128)(2,1)S(1)}, bf16[2,32,1536]{2,1,0:T(8,128)(2,1)S(1)}, u32[]{:S(2)}, u32[]{:S(2)}) %collective-permute-start.31) | collective-permute-done | bytes 196640 | tf_op jit(solution)/shard_map/ppermute | solution.py:38
  130.3 2.8 %collective-permute-start.36 = (f32[2,1536]{1,0:T(2,128)S(1)}, f32[2,1536]{1,0:T(2,128)S(1)}, u32[]{:S(2)}, u32[]{:S(2)}) collective-permute-start(f32[2,1536]{1,0:T(2,128)S(1)} %add.48), channel_id=1, source_target_pairs={{0,4},{1,5},{2,6},{3,7},{4,0},{5,1},{6,2},{7,3},{8,12},{9,13},{10,... | collective-permute-start | bytes 36872 | tf_op jit(solution)/shard_map/ppermute | solution.py:38
  133.1 1.5 collective-permute-start.35
  134.8 7.1 %collective-permute-start.33 = (bf16[32,1536]{1,0:T(8,128)(2,1)S(1)}, bf16[32,1536]{1,0:T(8,128)(2,1)S(1)}, u32[]{:S(2)}, u32[]{:S(2)}) collective-permute-start(bf16[32,1536]{1,0:T(8,128)(2,1)S(1)} %get-tuple-element.126), channel_id=1, source_target_pairs={{0,8},{8,16},{16,24},{24,32},{32,40},{40,48},{48,56},{56,64},{64,7... | collective-permute-start | bytes 294920 | tf_op jit(solution)/shard_map/ppermute | solution.py:351
  145.0 7.8 %collective-permute-done.34 = bf16[32,1536]{1,0:T(8,128)(2,1)S(1)} collective-permute-done((bf16[32,1536]{1,0:T(8,128)(2,1)S(1)}, bf16[32,1536]{1,0:T(8,128)(2,1)S(1)}, u32[]{:S(2)}, u32[]{:S(2)}) %collective-permute-start.34) | collective-permute-done | bytes 98336 | tf_op jit(solution)/shard_map/ppermute | solution.py:351
  (85 shorter events, 27.3 us)
Async XLA Ops:
  1.6 13.0 %collective-permute-start.3 = (bf16[2,32,1536]{2,1,0:T(8,128)(2,1)S(1)}, bf16[2,32,1536]{2,1,0:T(8,128)(2,1)S(1)}, u32[]{:S(2)}, u32[]{:S(2)}) collective-permute-start(bf16[2,32,1536]{2,1,0:T(8,128)(2,1)S(1)} %stack.1.own_b), channel_id=1, source_target_pairs={{0,1},{1,0},{2,3},{3,2},{4,5},{5,4},{6,7},{7,6},{8,9},{9,8},{10,11... | collective-permute-start | bytes 589832 | tf_op jit(solution)/shard_map/ppermute | solution.py:38
  4.9 15.8 %collective-permute-start = (bf16[2,32,1536]{2,1,0:T(8,128)(2,1)S(1)}, bf16[2,32,1536]{2,1,0:T(8,128)(2,1)S(1)}, u32[]{:S(2)}, u32[]{:S(2)}) collective-permute-start(bf16[2,32,1536]{2,1,0:T(8,128)(2,1)S(1)} %stack.1.own_b), channel_id=1, source_target_pairs={{0,2},{1,7},{2,4},{3,1},{4,6},{5,3},{6,0},{7,5},{8,10},{9,15},{10,... | collective-permute-start | bytes 589832 | tf_op jit(solution)/shard_map/ppermute | solution.py:38
  9.2 25.3 %collective-permute-start.5 = (bf16[2,256,384]{2,1,0:T(8,128)(2,1)}, bf16[2,256,384]{2,1,0:T(8,128)(2,1)S(1)}, u32[]{:S(2)}, u32[]{:S(2)}) collective-permute-start(bf16[2,256,384]{2,1,0:T(8,128)(2,1)} %bitcast.49), channel_id=1, source_target_pairs={{0,248},{8,240},{16,232},{24,224},{32,216},{40,208},{48,200},{56,1... | collective-permute-start | bytes 1179656 | tf_op jit(solution)/shard_map/ppermute | solution.py:356
  14.6 6.5 %collective-permute-start.4 = (bf16[2,32,1536]{2,1,0:T(8,128)(2,1)S(1)}, bf16[2,32,1536]{2,1,0:T(8,128)(2,1)S(1)}, u32[]{:S(2)}, u32[]{:S(2)}) collective-permute-start(bf16[2,32,1536]{2,1,0:T(8,128)(2,1)S(1)} %collective-permute-done.3.other), channel_id=1, source_target_pairs={{0,2},{1,7},{2,4},{3,1},{4,6},{5,3},{6,0},{7,5},{8,10},{9,15},{10,... | collective-permute-start | bytes 589832 | tf_op jit(solution)/shard_map/ppermute | solution.py:38
  20.7 11.1 %collective-permute-start.1 = (bf16[2,32,1536]{2,1,0:T(8,128)(2,1)S(1)}, bf16[2,32,1536]{2,1,0:T(8,128)(2,1)S(1)}, u32[]{:S(2)}, u32[]{:S(2)}) collective-permute-start(bf16[2,32,1536]{2,1,0:T(8,128)(2,1)S(1)} %collective-permute-done.near_0), channel_id=1, source_target_pairs={{0,2},{1,7},{2,4},{3,1},{4,6},{5,3},{6,0},{7,5},{8,10},{9,15},{10,... | collective-permute-start | bytes 589832 | tf_op jit(solution)/shard_map/ppermute | solution.py:38
  21.1 13.5 %collective-permute-start.7 = (bf16[2,32,1536]{2,1,0:T(8,128)(2,1)S(1)}, bf16[2,32,1536]{2,1,0:T(8,128)(2,1)S(1)}, u32[]{:S(2)}, u32[]{:S(2)}) collective-permute-start(bf16[2,32,1536]{2,1,0:T(8,128)(2,1)S(1)} %collective-permute-done.4.near_1), channel_id=1, source_target_pairs={{0,1},{1,0},{2,3},{3,2},{4,5},{5,4},{6,7},{7,6},{8,9},{9,8},{10,11... | collective-permute-start | bytes 589832 | tf_op jit(solution)/shard_map/ppermute | solution.py:38
  31.9 14.8 %collective-permute-start.2 = (bf16[1920,128]{1,0:T(8,128)(2,1)S(1)}, bf16[1920,128]{1,0:T(8,128)(2,1)S(1)}, u32[]{:S(2)}, u32[]{:S(2)}) collective-permute-start(bf16[1920,128]{1,0:T(8,128)(2,1)S(1)} %pack_held.1), channel_id=1, source_target_pairs={{0,248},{8,240},{16,232},{24,224},{32,216},{40,208},{48,200},{56,1... | collective-permute-start | bytes 1474568 | tf_op jit(solution)/shard_map/ppermute | solution.py:356
  46.7 4.1 %collective-permute-start.10 = (bf16[2,32,1536]{2,1,0:T(8,128)(2,1)S(1)}, bf16[2,32,1536]{2,1,0:T(8,128)(2,1)S(1)}, u32[]{:S(2)}, u32[]{:S(2)}) collective-permute-start(bf16[2,32,1536]{2,1,0:T(8,128)(2,1)S(1)} %get-tuple-element.89), channel_id=1, source_target_pairs={{0,1},{1,0},{2,3},{3,2},{4,5},{5,4},{6,7},{7,6},{8,9},{9,8},{10,11... | collective-permute-start | bytes 589832 | tf_op jit(solution)/shard_map/ppermute | solution.py:38
  51.3 3.4 %collective-permute-start.9 = (bf16[2,32,1536]{2,1,0:T(8,128)(2,1)S(1)}, bf16[2,32,1536]{2,1,0:T(8,128)(2,1)S(1)}, u32[]{:S(2)}, u32[]{:S(2)}) collective-permute-start(bf16[2,32,1536]{2,1,0:T(8,128)(2,1)S(1)} %get-tuple-element.86), channel_id=1, source_target_pairs={{0,1},{1,0},{2,3},{3,2},{4,5},{5,4},{6,7},{7,6},{8,9},{9,8},{10,11... | collective-permute-start | bytes 589832 | tf_op jit(solution)/shard_map/ppermute | solution.py:38
  51.4 8.0 %collective-permute-start.11 = (bf16[2,32,1536]{2,1,0:T(8,128)(2,1)S(1)}, bf16[2,32,1536]{2,1,0:T(8,128)(2,1)S(1)}, u32[]{:S(2)}, u32[]{:S(2)}) collective-permute-start(bf16[2,32,1536]{2,1,0:T(8,128)(2,1)S(1)} %add_convert_fusion.8), channel_id=1, source_target_pairs={{0,6},{1,3},{2,0},{3,5},{4,2},{5,7},{6,4},{7,1},{8,14},{9,11},{10,... | collective-permute-start | bytes 589832 | tf_op jit(solution)/shard_map/ppermute | solution.py:38
  52.4 12.1 %collective-permute-start.14 = (bf16[2,32,1536]{2,1,0:T(8,128)(2,1)S(1)}, bf16[2,32,1536]{2,1,0:T(8,128)(2,1)S(1)}, u32[]{:S(2)}, u32[]{:S(2)}) collective-permute-start(bf16[2,32,1536]{2,1,0:T(8,128)(2,1)S(1)} %add_convert_fusion.6), channel_id=1, source_target_pairs={{0,6},{1,3},{2,0},{3,5},{4,2},{5,7},{6,4},{7,1},{8,14},{9,11},{10,... | collective-permute-start | bytes 589832 | tf_op jit(solution)/shard_map/ppermute | solution.py:38
  59.5 9.2 %collective-permute-start.12 = (bf16[2,32,1536]{2,1,0:T(8,128)(2,1)S(1)}, bf16[2,32,1536]{2,1,0:T(8,128)(2,1)S(1)}, u32[]{:S(2)}, u32[]{:S(2)}) collective-permute-start(bf16[2,32,1536]{2,1,0:T(8,128)(2,1)S(1)} %add_convert_fusion.7), channel_id=1, source_target_pairs={{0,6},{1,3},{2,0},{3,5},{4,2},{5,7},{6,4},{7,1},{8,14},{9,11},{10,... | collective-permute-start | bytes 589832 | tf_op jit(solution)/shard_map/ppermute | solution.py:38
  64.6 4.1 %collective-permute-start.15 = (bf16[2,32,1536]{2,1,0:T(8,128)(2,1)S(1)}, bf16[2,32,1536]{2,1,0:T(8,128)(2,1)S(1)}, u32[]{:S(2)}, u32[]{:S(2)}) collective-permute-start(bf16[2,32,1536]{2,1,0:T(8,128)(2,1)S(1)} %add_convert_fusion.5), channel_id=1, source_target_pairs={{0,1},{1,0},{2,3},{3,2},{4,5},{5,4},{6,7},{7,6},{8,9},{9,8},{10,11... | collective-permute-start | bytes 589832 | tf_op jit(solution)/shard_map/ppermute | solution.py:38
  69.5 4.0 %collective-permute-start.16 = (bf16[4,32,1536]{2,1,0:T(8,128)(2,1)S(1)}, bf16[4,32,1536]{2,1,0:T(8,128)(2,1)S(1)}, u32[]{:S(2)}, u32[]{:S(2)}) collective-permute-start(bf16[4,32,1536]{2,1,0:T(8,128)(2,1)S(1)} %get-tuple-element.94.own_b.mids), channel_id=1, source_target_pairs={{0,1},{1,0},{2,3},{3,2},{4,5},{5,4},{6,7},{7,6},{8,9},{9,8},{10,11... | collective-permute-start | bytes 1179656 | tf_op jit(solution)/shard_map/ppermute | solution.py:38
  70.9 19.2 %collective-permute-start.17 = (bf16[4,32,1536]{2,1,0:T(8,128)(2,1)S(1)}, bf16[4,32,1536]{2,1,0:T(8,128)(2,1)S(1)}, u32[]{:S(2)}, u32[]{:S(2)}) collective-permute-start(bf16[4,32,1536]{2,1,0:T(8,128)(2,1)S(1)} %get-tuple-element.94.own_b.mids), channel_id=1, source_target_pairs={{0,2},{1,7},{2,4},{3,1},{4,6},{5,3},{6,0},{7,5},{8,10},{9,15},{10,... | collective-permute-start | bytes 1179656 | tf_op jit(solution)/shard_map/ppermute | solution.py:38
  73.5 20.8 %collective-permute-start.18 = (bf16[4,32,1536]{2,1,0:T(8,128)(2,1)S(1)}, bf16[4,32,1536]{2,1,0:T(8,128)(2,1)S(1)}, u32[]{:S(2)}, u32[]{:S(2)}) collective-permute-start(bf16[4,32,1536]{2,1,0:T(8,128)(2,1)S(1)} %collective-permute-done.16.other), channel_id=1, source_target_pairs={{0,2},{1,7},{2,4},{3,1},{4,6},{5,3},{6,0},{7,5},{8,10},{9,15},{10,... | collective-permute-start | bytes 1179656 | tf_op jit(solution)/shard_map/ppermute | solution.py:38
  90.1 8.4 %collective-permute-start.19 = (bf16[4,32,1536]{2,1,0:T(8,128)(2,1)S(1)}, bf16[4,32,1536]{2,1,0:T(8,128)(2,1)S(1)}, u32[]{:S(2)}, u32[]{:S(2)}) collective-permute-start(bf16[4,32,1536]{2,1,0:T(8,128)(2,1)S(1)} %collective-permute-done.17.near_0), channel_id=1, source_target_pairs={{0,2},{1,7},{2,4},{3,1},{4,6},{5,3},{6,0},{7,5},{8,10},{9,15},{10,... | collective-permute-start | bytes 1179656 | tf_op jit(solution)/shard_map/ppermute | solution.py:38
  94.3 4.2 %collective-permute-start.21 = (bf16[4,32,1536]{2,1,0:T(8,128)(2,1)S(1)}, bf16[4,32,1536]{2,1,0:T(8,128)(2,1)S(1)}, u32[]{:S(2)}, u32[]{:S(2)}) collective-permute-start(bf16[4,32,1536]{2,1,0:T(8,128)(2,1)S(1)} %collective-permute-done.18.near_1), channel_id=1, source_target_pairs={{0,1},{1,0},{2,3},{3,2},{4,5},{5,4},{6,7},{7,6},{8,9},{9,8},{10,11... | collective-permute-start | bytes 1179656 | tf_op jit(solution)/shard_map/ppermute | solution.py:38
  96.0 17.2 %collective-permute-start.24 = (bf16[1920,128]{1,0:T(8,128)(2,1)S(1)}, bf16[1920,128]{1,0:T(8,128)(2,1)S(1)}, u32[]{:S(2)}, u32[]{:S(2)}) collective-permute-start(bf16[1920,128]{1,0:T(8,128)(2,1)S(1)} %pack_new.1), channel_id=1, source_target_pairs={{0,248},{8,240},{16,232},{24,224},{32,216},{40,208},{48,200},{56,1... | collective-permute-start | bytes 1474568 | tf_op jit(solution)/shard_map/ppermute | solution.py:356
  96.1 6.2 %collective-permute-start.20 = (bf16[4,32,1536]{2,1,0:T(8,128)(2,1)S(1)}, bf16[4,32,1536]{2,1,0:T(8,128)(2,1)S(1)}, u32[]{:S(2)}, u32[]{:S(2)}) collective-permute-start(bf16[4,32,1536]{2,1,0:T(8,128)(2,1)S(1)} %collective-permute-done.17.near_0), channel_id=1, source_target_pairs={{0,1},{1,0},{2,3},{3,2},{4,5},{5,4},{6,7},{7,6},{8,9},{9,8},{10,11... | collective-permute-start | bytes 1179656 | tf_op jit(solution)/shard_map/ppermute | solution.py:38
  98.5 5.1 %collective-permute-start.22 = (bf16[4,32,1536]{2,1,0:T(8,128)(2,1)S(1)}, bf16[4,32,1536]{2,1,0:T(8,128)(2,1)S(1)}, u32[]{:S(2)}, u32[]{:S(2)}) collective-permute-start(bf16[4,32,1536]{2,1,0:T(8,128)(2,1)S(1)} %collective-permute-done.19.far), channel_id=1, source_target_pairs={{0,1},{1,0},{2,3},{3,2},{4,5},{5,4},{6,7},{7,6},{8,9},{9,8},{10,11... | collective-permute-start | bytes 1179656 | tf_op jit(solution)/shard_map/ppermute | solution.py:38
  115.0 4.9 %collective-permute-start.30 = (bf16[2,32,1536]{2,1,0:T(8,128)(2,1)S(1)}, bf16[2,32,1536]{2,1,0:T(8,128)(2,1)S(1)}, u32[]{:S(2)}, u32[]{:S(2)}) collective-permute-start(bf16[2,32,1536]{2,1,0:T(8,128)(2,1)S(1)} %get-tuple-element.125), channel_id=1, source_target_pairs={{0,1},{1,0},{2,3},{3,2},{4,5},{5,4},{6,7},{7,6},{8,9},{9,8},{10,11... | collective-permute-start | bytes 589832 | tf_op jit(solution)/shard_map/ppermute | solution.py:38
  115.5 4.4 %collective-permute-start.28 = (f32[2,1536]{1,0:T(2,128)S(1)}, f32[2,1536]{1,0:T(2,128)S(1)}, u32[]{:S(2)}, u32[]{:S(2)}) collective-permute-start(f32[2,1536]{1,0:T(2,128)S(1)} %fusion), channel_id=1, source_target_pairs={{0,2},{1,3},{2,0},{3,1},{4,6},{5,7},{6,4},{7,5},{8,10},{9,11},{10,... | collective-permute-start | bytes 36872 | tf_op jit(solution)/shard_map/ppermute | solution.py:38
  117.1 5.3 %collective-permute-start.23 = (bf16[2,32,1536]{2,1,0:T(8,128)(2,1)S(1)}, bf16[2,32,1536]{2,1,0:T(8,128)(2,1)S(1)}, u32[]{:S(2)}, u32[]{:S(2)}) collective-permute-start(bf16[2,32,1536]{2,1,0:T(8,128)(2,1)S(1)} %get-tuple-element.101), channel_id=1, source_target_pairs={{0,1},{1,0},{2,3},{3,2},{4,5},{5,4},{6,7},{7,6},{8,9},{9,8},{10,11... | collective-permute-start | bytes 589832 | tf_op jit(solution)/shard_map/ppermute | solution.py:38
  117.5 8.3 %collective-permute-start.26 = (bf16[2,32,1536]{2,1,0:T(8,128)(2,1)S(1)}, bf16[2,32,1536]{2,1,0:T(8,128)(2,1)S(1)}, u32[]{:S(2)}, u32[]{:S(2)}) collective-permute-start(bf16[2,32,1536]{2,1,0:T(8,128)(2,1)S(1)} %add_convert_fusion.3), channel_id=1, source_target_pairs={{0,6},{1,3},{2,0},{3,5},{4,2},{5,7},{6,4},{7,1},{8,14},{9,11},{10,... | collective-permute-start | bytes 589832 | tf_op jit(solution)/shard_map/ppermute | solution.py:38
  120.0 10.2 %collective-permute-start.31 = (bf16[2,32,1536]{2,1,0:T(8,128)(2,1)S(1)}, bf16[2,32,1536]{2,1,0:T(8,128)(2,1)S(1)}, u32[]{:S(2)}, u32[]{:S(2)}) collective-permute-start(bf16[2,32,1536]{2,1,0:T(8,128)(2,1)S(1)} %add_convert_fusion.1), channel_id=1, source_target_pairs={{0,6},{1,3},{2,0},{3,5},{4,2},{5,7},{6,4},{7,1},{8,14},{9,11},{10,... | collective-permute-start | bytes 589832 | tf_op jit(solution)/shard_map/ppermute | solution.py:38
  125.9 8.6 %collective-permute-start.29 = (bf16[2,32,1536]{2,1,0:T(8,128)(2,1)S(1)}, bf16[2,32,1536]{2,1,0:T(8,128)(2,1)S(1)}, u32[]{:S(2)}, u32[]{:S(2)}) collective-permute-start(bf16[2,32,1536]{2,1,0:T(8,128)(2,1)S(1)} %add_convert_fusion.2), channel_id=1, source_target_pairs={{0,6},{1,3},{2,0},{3,5},{4,2},{5,7},{6,4},{7,1},{8,14},{9,11},{10,... | collective-permute-start | bytes 589832 | tf_op jit(solution)/shard_map/ppermute | solution.py:38
  130.2 4.4 %collective-permute-start.32 = (bf16[2,32,1536]{2,1,0:T(8,128)(2,1)S(1)}, bf16[2,32,1536]{2,1,0:T(8,128)(2,1)S(1)}, u32[]{:S(2)}, u32[]{:S(2)}) collective-permute-start(bf16[2,32,1536]{2,1,0:T(8,128)(2,1)S(1)} %add_convert_fusion), channel_id=1, source_target_pairs={{0,1},{1,0},{2,3},{3,2},{4,5},{5,4},{6,7},{7,6},{8,9},{9,8},{10,11... | collective-permute-start | bytes 589832 | tf_op jit(solution)/shard_map/ppermute | solution.py:38
  130.3 12.9 %collective-permute-start.36 = (f32[2,1536]{1,0:T(2,128)S(1)}, f32[2,1536]{1,0:T(2,128)S(1)}, u32[]{:S(2)}, u32[]{:S(2)}) collective-permute-start(f32[2,1536]{1,0:T(2,128)S(1)} %add.48), channel_id=1, source_target_pairs={{0,4},{1,5},{2,6},{3,7},{4,0},{5,1},{6,2},{7,3},{8,12},{9,13},{10,... | collective-permute-start | bytes 36872 | tf_op jit(solution)/shard_map/ppermute | solution.py:38
  133.1 19.8 %collective-permute-start.35 = (bf16[2,256,384]{2,1,0:T(8,128)(2,1)S(1)}, bf16[2,256,384]{2,1,0:T(8,128)(2,1)S(1)}, u32[]{:S(2)}, u32[]{:S(2)}) collective-permute-start(bf16[2,256,384]{2,1,0:T(8,128)(2,1)S(1)} %get-tuple-element.129.kept), channel_id=1, source_target_pairs={{0,248},{8,240},{16,232},{24,224},{32,216},{40,208},{48,200},{56,1... | collective-permute-start | bytes 1179656 | tf_op jit(solution)/shard_map/ppermute | solution.py:356
  134.8 10.2 %collective-permute-start.33 = (bf16[32,1536]{1,0:T(8,128)(2,1)S(1)}, bf16[32,1536]{1,0:T(8,128)(2,1)S(1)}, u32[]{:S(2)}, u32[]{:S(2)}) collective-permute-start(bf16[32,1536]{1,0:T(8,128)(2,1)S(1)} %get-tuple-element.126), channel_id=1, source_target_pairs={{0,8},{8,16},{16,24},{24,32},{32,40},{40,48},{48,56},{56,64},{64,7... | collective-permute-start | bytes 294920 | tf_op jit(solution)/shard_map/ppermute | solution.py:351
  141.9 10.9 %collective-permute-start.34 = (bf16[32,1536]{1,0:T(8,128)(2,1)S(1)}, bf16[32,1536]{1,0:T(8,128)(2,1)S(1)}, u32[]{:S(2)}, u32[]{:S(2)}) collective-permute-start(bf16[32,1536]{1,0:T(8,128)(2,1)S(1)} %get-tuple-element.127), channel_id=1, source_target_pairs={{8,0},{16,8},{24,16},{32,24},{40,32},{48,40},{56,48},{64,56},{72,6... | collective-permute-start | bytes 294920 | tf_op jit(solution)/shard_map/ppermute | solution.py:351
  (13 other events, 154.4 us)

commit v2 on v1

--- a/solution.py
+++ b/solution.py
@@ -380,7 +380,7 @@
     )
     (packed,) = call(pack_held, "pack_held", [shape(STASH, 128)], [], 8192, (held_x, after(held_q, own)))
     blocks = gather(own, (wqkv, packed), lambda _: (fetched_g,))
-    fetched = mirrored(after(packed, blocks[4]))
+    fetched = mirrored(after(packed, blocks[3]))
 
     qkv, dgateup, act_low, grads, *parts = call(
         first_stage, "first_stage",

time: 156 us -> 153 us (0.981)
  starting transfers between devices: 69.6 us -> 65.4 us
    ppermute x4, waiting for transfers between devices: 5.91 us -> 10.7 us  [mirrored(): lax.ppermute(value, 'section', [(i, count - 1 - i) for i in range(count)])]
    ppermute x31, starting transfers between devices: 51.6 us -> 47.2 us  [over(): return lax.ppermute(value, 'tensor', pairs)]
    ppermute x4, starting transfers between devices: 9.64 us -> 13.3 us  [mirrored(): lax.ppermute(value, 'section', [(i, count - 1 - i) for i in range(count)])]
    ppermute x2, starting transfers between devices: 8.4 us -> 4.84 us  [shifted(): return lax.ppermute(value, 'section', pairs)]
    ppermute x31, waiting for transfers between devices: 42.4 us -> 39.8 us  [over(): return lax.ppermute(value, 'tensor', pairs)]
  transfers between devices with their start and end apart: 37 -> 37, of which waited for: 18 -> 17; matrix products, arithmetic and copies ran while one was open for 1% -> 1% of each run, Pallas kernels for 13% -> 13%
where the time goes in v2:
time: 153 us
  starting transfers between devices  65.4 us (43%)
  waiting for transfers between devices  58.8 us (38%)
  Pallas kernels  23.3 us (15%)
  local copies, waits for them, and re-layouts  3.21 us (2%)
    ppermute x31, starting transfers between devices, over(): return lax.ppermute(value, 'tensor', pairs)  47.2 us
    ppermute x31, waiting for transfers between devices, over(): return lax.ppermute(value, 'tensor', pairs)  39.8 us
    pallas_call x13, Pallas kernels, call(): pl.pallas_call(body, name=name, out_shape=outs, in_specs=[hbm if i in str...  23.3 us
    ppermute x4, starting transfers between devices, mirrored(): lax.ppermute(value, 'section', [(i, count - 1 - i) for i in range(count)])  13.3 us
    ppermute x4, waiting for transfers between devices, mirrored(): lax.ppermute(value, 'section', [(i, count - 1 - i) for i in range(count)])  10.7 us
    ppermute x2, waiting for transfers between devices, shifted(): return lax.ppermute(value, 'section', pairs)  8.33 us
    ppermute x2, starting transfers between devices, shifted(): return lax.ppermute(value, 'section', pairs)  4.84 us
    unnamed x18, local copies, waits for them, and re-layouts  3.21 us
  transfers between devices with their start and end apart: 37, of which 17 were waited for; matrix products, arithmetic and copies ran while one was open for 1% of the time, Pallas kernels for 13%

profile of v2, /device:TPU:1, one launch (start us, length us, event | category | flops | bytes accessed | tf_op | source)
XLA Modules:
  0.0 152.7 jit_solution(11093370242985643584)
XLA Ops:
  1.6 3.3 %collective-permute-start = (bf16[2,32,1536]{2,1,0:T(8,128)(2,1)S(1)}, bf16[2,32,1536]{2,1,0:T(8,128)(2,1)S(1)}, u32[]{:S(2)}, u32[]{:S(2)}) collective-permute-start(bf16[2,32,1536]{2,1,0:T(8,128)(2,1)S(1)} %stack.1.own_b), channel_id=1, source_target_pairs={{0,1},{1,0},{2,3},{3,2},{4,5},{5,4},{6,7},{7,6},{8,9},{9,8},{10,11... | collective-permute-start | bytes 589832 | tf_op jit(solution)/shard_map/ppermute | solution.py:38
  4.9 4.3 %collective-permute-start.3 = (bf16[2,32,1536]{2,1,0:T(8,128)(2,1)S(1)}, bf16[2,32,1536]{2,1,0:T(8,128)(2,1)S(1)}, u32[]{:S(2)}, u32[]{:S(2)}) collective-permute-start(bf16[2,32,1536]{2,1,0:T(8,128)(2,1)S(1)} %stack.1.own_b), channel_id=1, source_target_pairs={{0,2},{1,7},{2,4},{3,1},{4,6},{5,3},{6,0},{7,5},{8,10},{9,15},{10,... | collective-permute-start | bytes 589832 | tf_op jit(solution)/shard_map/ppermute | solution.py:38
  9.2 5.4 %collective-permute-start.5 = (bf16[2,256,384]{2,1,0:T(8,128)(2,1)}, bf16[2,256,384]{2,1,0:T(8,128)(2,1)S(1)}, u32[]{:S(2)}, u32[]{:S(2)}) collective-permute-start(bf16[2,256,384]{2,1,0:T(8,128)(2,1)} %bitcast.49), channel_id=1, source_target_pairs={{0,248},{8,240},{16,232},{24,224},{32,216},{40,208},{48,200},{56,1... | collective-permute-start | bytes 1179656 | tf_op jit(solution)/shard_map/ppermute | solution.py:356
  17.8 2.9 %bring.1 = (bf16[3,192,1536]{2,1,0:T(8,128)(2,1)S(1)}, bf16[192,1536]{1,0:T(8,128)(2,1)S(1)}, bf16[2,256,384]{2,1,0:T(8,128)(2,1)S(1)}, bf16[384,1536]{1,0:T(8,128)(2,1)S(1)}, bf16[2,1536,384]{2,1,0:T(8,128)(2,1)S(1)}) custom-call(bf16[3,192,1536]{2,1,0:T(8,128)(2,1)} %bitcast.46, bf16[192,1536]{1,0:T(8,128)(2,1)} %bitcast.48, ...), custom_call_target="tpu_custom_call" | custom-call | flops 8192 | bytes 12582912 | tf_op jit(solution)/shard_map/bring/pallas_call | solution.py:84
  21.1 10.8 %collective-permute-start.7 = (bf16[2,32,1536]{2,1,0:T(8,128)(2,1)S(1)}, bf16[2,32,1536]{2,1,0:T(8,128)(2,1)S(1)}, u32[]{:S(2)}, u32[]{:S(2)}) collective-permute-start(bf16[2,32,1536]{2,1,0:T(8,128)(2,1)S(1)} %collective-permute-done.1.near_1), channel_id=1, source_target_pairs={{0,1},{1,0},{2,3},{3,2},{4,5},{5,4},{6,7},{7,6},{8,9},{9,8},{10,11... | collective-permute-start | bytes 589832 | tf_op jit(solution)/shard_map/ppermute | solution.py:38
  35.0 4.6 %first_stage.1 = (bf16[3,192,256]{2,1,0:T(8,128)(2,1)S(1)}, bf16[2,256,384]{2,1,0:T(8,128)(2,1)S(1)}, bf16[256,384]{1,0:T(8,128)(2,1)S(1)}, bf16[256,1536]{1,0:T...) custom-call(s32[16]{0:T(128)S(1)} %copy-done.7, ...), custom_call_target="tpu_custom_call" | custom-call | flops 1612185600 | bytes 11513920 | tf_op jit(solution)/shard_map/first_stage/pallas_call | solution.py:84
  39.6 9.3 %collective-permute-done.2.fetched = bf16[1920,128]{1,0:T(8,128)(2,1)S(1)} collective-permute-done((bf16[1920,128]{1,0:T(8,128)(2,1)S(1)}, bf16[1920,128]{1,0:T(8,128)(2,1)S(1)}, u32[]{:S(2)}, u32[]{:S(2)}) %collective-permute-start.2) | collective-permute-done | bytes 491552 | tf_op jit(solution)/shard_map/ppermute | solution.py:356
  52.4 2.3 %collective-permute-start.14 = (bf16[2,32,1536]{2,1,0:T(8,128)(2,1)S(1)}, bf16[2,32,1536]{2,1,0:T(8,128)(2,1)S(1)}, u32[]{:S(2)}, u32[]{:S(2)}) collective-permute-start(bf16[2,32,1536]{2,1,0:T(8,128)(2,1)S(1)} %add_convert_fusion.6), channel_id=1, source_target_pairs={{0,6},{1,3},{2,0},{3,5},{4,2},{5,7},{6,4},{7,1},{8,14},{9,11},{10,... | collective-permute-start | bytes 589832 | tf_op jit(solution)/shard_map/ppermute | solution.py:38
  54.8 6.8 %collective-permute-done.11 = bf16[2,32,1536]{2,1,0:T(8,128)(2,1)S(1)} collective-permute-done((bf16[2,32,1536]{2,1,0:T(8,128)(2,1)S(1)}, bf16[2,32,1536]{2,1,0:T(8,128)(2,1)S(1)}, u32[]{:S(2)}, u32[]{:S(2)}) %collective-permute-start.11) | collective-permute-done | bytes 196640 | tf_op jit(solution)/shard_map/ppermute | solution.py:38
  62.2 1.6 %collective-permute-done.14 = bf16[2,32,1536]{2,1,0:T(8,128)(2,1)S(1)} collective-permute-done((bf16[2,32,1536]{2,1,0:T(8,128)(2,1)S(1)}, bf16[2,32,1536]{2,1,0:T(8,128)(2,1)S(1)}, u32[]{:S(2)}, u32[]{:S(2)}) %collective-permute-start.14) | collective-permute-done | bytes 196640 | tf_op jit(solution)/shard_map/ppermute | solution.py:38
  65.0 3.6 %collective-permute-done.12.near = bf16[2,32,1536]{2,1,0:T(8,128)(2,1)S(1)} collective-permute-done((bf16[2,32,1536]{2,1,0:T(8,128)(2,1)S(1)}, bf16[2,32,1536]{2,1,0:T(8,128)(2,1)S(1)}, u32[]{:S(2)}, u32[]{:S(2)}) %collective-permute-start.12) | collective-permute-done | bytes 196640 | tf_op jit(solution)/shard_map/ppermute | solution.py:38
  69.5 1.5 collective-permute-start.16
  70.9 2.4 %collective-permute-start.17 = (bf16[4,32,1536]{2,1,0:T(8,128)(2,1)S(1)}, bf16[4,32,1536]{2,1,0:T(8,128)(2,1)S(1)}, u32[]{:S(2)}, u32[]{:S(2)}) collective-permute-start(bf16[4,32,1536]{2,1,0:T(8,128)(2,1)S(1)} %get-tuple-element.94.own_b.mids), channel_id=1, source_target_pairs={{0,2},{1,7},{2,4},{3,1},{4,6},{5,3},{6,0},{7,5},{8,10},{9,15},{10,... | collective-permute-start | bytes 1179656 | tf_op jit(solution)/shard_map/ppermute | solution.py:38
  76.0 13.4 %collective-permute-done.17.near_0 = bf16[4,32,1536]{2,1,0:T(8,128)(2,1)S(1)} collective-permute-done((bf16[4,32,1536]{2,1,0:T(8,128)(2,1)S(1)}, bf16[4,32,1536]{2,1,0:T(8,128)(2,1)S(1)}, u32[]{:S(2)}, u32[]{:S(2)}) %collective-permute-start.17) | collective-permute-done | bytes 393248 | tf_op jit(solution)/shard_map/ppermute | solution.py:38
  89.4 2.8 %collective-permute-start.19 = (bf16[4,32,1536]{2,1,0:T(8,128)(2,1)S(1)}, bf16[4,32,1536]{2,1,0:T(8,128)(2,1)S(1)}, u32[]{:S(2)}, u32[]{:S(2)}) collective-permute-start(bf16[4,32,1536]{2,1,0:T(8,128)(2,1)S(1)} %collective-permute-done.17.near_0), channel_id=1, source_target_pairs={{0,2},{1,7},{2,4},{3,1},{4,6},{5,3},{6,0},{7,5},{8,10},{9,15},{10,... | collective-permute-start | bytes 1179656 | tf_op jit(solution)/shard_map/ppermute | solution.py:38
  92.2 1.4 collective-permute-done.18.near_1
  93.6 1.8 %collective-permute-start.21 = (bf16[4,32,1536]{2,1,0:T(8,128)(2,1)S(1)}, bf16[4,32,1536]{2,1,0:T(8,128)(2,1)S(1)}, u32[]{:S(2)}, u32[]{:S(2)}) collective-permute-start(bf16[4,32,1536]{2,1,0:T(8,128)(2,1)S(1)} %collective-permute-done.18.near_1), channel_id=1, source_target_pairs={{0,1},{1,0},{2,3},{3,2},{4,5},{5,4},{6,7},{7,6},{8,9},{9,8},{10,11... | collective-permute-start | bytes 1179656 | tf_op jit(solution)/shard_map/ppermute | solution.py:38
  95.5 2.7 %collective-permute-start.24 = (bf16[1920,128]{1,0:T(8,128)(2,1)S(1)}, bf16[1920,128]{1,0:T(8,128)(2,1)S(1)}, u32[]{:S(2)}, u32[]{:S(2)}) collective-permute-start(bf16[1920,128]{1,0:T(8,128)(2,1)S(1)} %pack_new.1), channel_id=1, source_target_pairs={{0,248},{8,240},{16,232},{24,224},{32,216},{40,208},{48,200},{56,1... | collective-permute-start | bytes 1474568 | tf_op jit(solution)/shard_map/ppermute | solution.py:356
  99.0 1.5 collective-permute-start.22
  101.9 4.1 %second_stage.1 = (bf16[2,256,384]{2,1,0:T(8,128)(2,1)S(1)}, bf16[3,192,256]{2,1,0:T(8,128)(2,1)S(1)}, bf16[256,1536]{1,0:T(8,128)(2,1)S(1)}, bf16[2,32,1536]{2,...) custom-call(bf16[4,32,1536]{2,1,0:T(8,128)(2,1)S(1)} %get-tuple-elem, ...), custom_call_target="tpu_custom_call" | custom-call | flops 1024 | bytes 1024 | tf_op jit(solution)/shard_map/second_stage/pallas_call | solution.py:84
  105.9 2.3 %attention_weights.1 = (bf16[3,192,1536]{2,1,0:T(8,128)(2,1)}, bf16[192,1536]{1,0:T(8,128)(2,1)}, f32[1,1536]{1,0:T(1,128)S(1)}) custom-call(bf16[4,32,1536]{2,1,0:T(8,128)(2,1)S(1)} %get-tuple-element.94.own_b.mids, bf16[4,32,1536]{2,1,0:T(8,128)(2,1)S(1)} %collective-permute-done.16.other, bf16[4,32,1536]{2,1,0:T(8,128)(2,1)S(1)} %collective-permute-done.17.near_0, ...), custom_call_target="tpu_custom_call" | custom-call | flops 1024 | bytes 1024 | tf_op jit(solution)/shard_map/attention_weights/pallas_call | solution.py:84
  108.3 3.0 %mlp_weights.1 = (bf16[2,1536,384]{2,1,0:T(8,128)(2,1)}, bf16[384,1536]{1,0:T(8,128)(2,1)}) custom-call(bf16[4,32,1536]{2,1,0:T(8,128)(2,1)S(1)} %get-tuple-element.94.own_b.mids, bf16[4,32,1536]{2,1,0:T(8,128)(2,1)S(1)} %collective-permute-done.16.other, bf16[4,32,1536]{2,1,0:T(8,128)(2,1)S(1)} %collective-permute-done.17.near_0, ...), custom_call_target="tpu_custom_call" | custom-call | flops 1024 | bytes 1024 | tf_op jit(solution)/shard_map/mlp_weights/pallas_call | solution.py:84
  111.3 1.4 collective-permute-done.24.packed
  116.5 1.4 collective-permute-start.26
  117.9 1.5 stash_out.1
  120.8 4.0 %collective-permute-done.26 = bf16[2,32,1536]{2,1,0:T(8,128)(2,1)S(1)} collective-permute-done((bf16[2,32,1536]{2,1,0:T(8,128)(2,1)S(1)}, bf16[2,32,1536]{2,1,0:T(8,128)(2,1)S(1)}, u32[]{:S(2)}, u32[]{:S(2)}) %collective-permute-start.26) | collective-permute-done | bytes 196640 | tf_op jit(solution)/shard_map/ppermute | solution.py:38
  125.0 4.0 %collective-permute-done.31 = bf16[2,32,1536]{2,1,0:T(8,128)(2,1)S(1)} collective-permute-done((bf16[2,32,1536]{2,1,0:T(8,128)(2,1)S(1)}, bf16[2,32,1536]{2,1,0:T(8,128)(2,1)S(1)}, u32[]{:S(2)}, u32[]{:S(2)}) %collective-permute-start.31) | collective-permute-done | bytes 196640 | tf_op jit(solution)/shard_map/ppermute | solution.py:38
  129.2 2.2 %collective-permute-start.36 = (f32[2,1536]{1,0:T(2,128)S(1)}, f32[2,1536]{1,0:T(2,128)S(1)}, u32[]{:S(2)}, u32[]{:S(2)}) collective-permute-start(f32[2,1536]{1,0:T(2,128)S(1)} %add.48), channel_id=1, source_target_pairs={{0,4},{1,5},{2,6},{3,7},{4,0},{5,1},{6,2},{7,3},{8,12},{9,13},{10,... | collective-permute-start | bytes 36872 | tf_op jit(solution)/shard_map/ppermute | solution.py:38
  131.4 4.6 %collective-permute-start.35 = (bf16[2,256,384]{2,1,0:T(8,128)(2,1)S(1)}, bf16[2,256,384]{2,1,0:T(8,128)(2,1)S(1)}, u32[]{:S(2)}, u32[]{:S(2)}) collective-permute-start(bf16[2,256,384]{2,1,0:T(8,128)(2,1)S(1)} %get-tuple-element.129.kept), channel_id=1, source_target_pairs={{0,248},{8,240},{16,232},{24,224},{32,216},{40,208},{48,200},{56,1... | collective-permute-start | bytes 1179656 | tf_op jit(solution)/shard_map/ppermute | solution.py:356
  136.2 3.6 %collective-permute-start.33 = (bf16[32,1536]{1,0:T(8,128)(2,1)S(1)}, bf16[32,1536]{1,0:T(8,128)(2,1)S(1)}, u32[]{:S(2)}, u32[]{:S(2)}) collective-permute-start(bf16[32,1536]{1,0:T(8,128)(2,1)S(1)} %get-tuple-element.126), channel_id=1, source_target_pairs={{0,8},{8,16},{16,24},{24,32},{32,40},{40,48},{48,56},{56,64},{64,7... | collective-permute-start | bytes 294920 | tf_op jit(solution)/shard_map/ppermute | solution.py:351
  141.7 4.6 %collective-permute-done.33 = bf16[32,1536]{1,0:T(8,128)(2,1)S(1)} collective-permute-done((bf16[32,1536]{1,0:T(8,128)(2,1)S(1)}, bf16[32,1536]{1,0:T(8,128)(2,1)S(1)}, u32[]{:S(2)}, u32[]{:S(2)}) %collective-permute-start.33) | collective-permute-done | bytes 98336 | tf_op jit(solution)/shard_map/ppermute | solution.py:351
  146.3 3.8 %collective-permute-done.34 = bf16[32,1536]{1,0:T(8,128)(2,1)S(1)} collective-permute-done((bf16[32,1536]{1,0:T(8,128)(2,1)S(1)}, bf16[32,1536]{1,0:T(8,128)(2,1)S(1)}, u32[]{:S(2)}, u32[]{:S(2)}) %collective-permute-start.34) | collective-permute-done | bytes 98336 | tf_op jit(solution)/shard_map/ppermute | solution.py:351
  (85 shorter events, 29.2 us)
Async XLA Ops:
  1.6 13.0 %collective-permute-start = (bf16[2,32,1536]{2,1,0:T(8,128)(2,1)S(1)}, bf16[2,32,1536]{2,1,0:T(8,128)(2,1)S(1)}, u32[]{:S(2)}, u32[]{:S(2)}) collective-permute-start(bf16[2,32,1536]{2,1,0:T(8,128)(2,1)S(1)} %stack.1.own_b), channel_id=1, source_target_pairs={{0,1},{1,0},{2,3},{3,2},{4,5},{5,4},{6,7},{7,6},{8,9},{9,8},{10,11... | collective-permute-start | bytes 589832 | tf_op jit(solution)/shard_map/ppermute | solution.py:38
  4.9 15.8 %collective-permute-start.3 = (bf16[2,32,1536]{2,1,0:T(8,128)(2,1)S(1)}, bf16[2,32,1536]{2,1,0:T(8,128)(2,1)S(1)}, u32[]{:S(2)}, u32[]{:S(2)}) collective-permute-start(bf16[2,32,1536]{2,1,0:T(8,128)(2,1)S(1)} %stack.1.own_b), channel_id=1, source_target_pairs={{0,2},{1,7},{2,4},{3,1},{4,6},{5,3},{6,0},{7,5},{8,10},{9,15},{10,... | collective-permute-start | bytes 589832 | tf_op jit(solution)/shard_map/ppermute | solution.py:38
  9.2 23.2 %collective-permute-start.5 = (bf16[2,256,384]{2,1,0:T(8,128)(2,1)}, bf16[2,256,384]{2,1,0:T(8,128)(2,1)S(1)}, u32[]{:S(2)}, u32[]{:S(2)}) collective-permute-start(bf16[2,256,384]{2,1,0:T(8,128)(2,1)} %bitcast.49), channel_id=1, source_target_pairs={{0,248},{8,240},{16,232},{24,224},{32,216},{40,208},{48,200},{56,1... | collective-permute-start | bytes 1179656 | tf_op jit(solution)/shard_map/ppermute | solution.py:356
  14.6 6.5 %collective-permute-start.1 = (bf16[2,32,1536]{2,1,0:T(8,128)(2,1)S(1)}, bf16[2,32,1536]{2,1,0:T(8,128)(2,1)S(1)}, u32[]{:S(2)}, u32[]{:S(2)}) collective-permute-start(bf16[2,32,1536]{2,1,0:T(8,128)(2,1)S(1)} %collective-permute-done.other), channel_id=1, source_target_pairs={{0,2},{1,7},{2,4},{3,1},{4,6},{5,3},{6,0},{7,5},{8,10},{9,15},{10,... | collective-permute-start | bytes 589832 | tf_op jit(solution)/shard_map/ppermute | solution.py:38
  20.7 12.5 %collective-permute-start.4 = (bf16[2,32,1536]{2,1,0:T(8,128)(2,1)S(1)}, bf16[2,32,1536]{2,1,0:T(8,128)(2,1)S(1)}, u32[]{:S(2)}, u32[]{:S(2)}) collective-permute-start(bf16[2,32,1536]{2,1,0:T(8,128)(2,1)S(1)} %collective-permute-done.3.near_0), channel_id=1, source_target_pairs={{0,2},{1,7},{2,4},{3,1},{4,6},{5,3},{6,0},{7,5},{8,10},{9,15},{10,... | collective-permute-start | bytes 589832 | tf_op jit(solution)/shard_map/ppermute | solution.py:38
  21.1 12.2 %collective-permute-start.7 = (bf16[2,32,1536]{2,1,0:T(8,128)(2,1)S(1)}, bf16[2,32,1536]{2,1,0:T(8,128)(2,1)S(1)}, u32[]{:S(2)}, u32[]{:S(2)}) collective-permute-start(bf16[2,32,1536]{2,1,0:T(8,128)(2,1)S(1)} %collective-permute-done.1.near_1), channel_id=1, source_target_pairs={{0,1},{1,0},{2,3},{3,2},{4,5},{5,4},{6,7},{7,6},{8,9},{9,8},{10,11... | collective-permute-start | bytes 589832 | tf_op jit(solution)/shard_map/ppermute | solution.py:38
  31.9 17.1 %collective-permute-start.2 = (bf16[1920,128]{1,0:T(8,128)(2,1)S(1)}, bf16[1920,128]{1,0:T(8,128)(2,1)S(1)}, u32[]{:S(2)}, u32[]{:S(2)}) collective-permute-start(bf16[1920,128]{1,0:T(8,128)(2,1)S(1)} %pack_held.1), channel_id=1, source_target_pairs={{0,248},{8,240},{16,232},{24,224},{32,216},{40,208},{48,200},{56,1... | collective-permute-start | bytes 1474568 | tf_op jit(solution)/shard_map/ppermute | solution.py:356
  32.4 1.9 %collective-permute-start.6 = (bf16[2,32,1536]{2,1,0:T(8,128)(2,1)S(1)}, bf16[2,32,1536]{2,1,0:T(8,128)(2,1)S(1)}, u32[]{:S(2)}, u32[]{:S(2)}) collective-permute-start(bf16[2,32,1536]{2,1,0:T(8,128)(2,1)S(1)} %collective-permute-done.3.near_0), channel_id=1, source_target_pairs={{0,1},{1,0},{2,3},{3,2},{4,5},{5,4},{6,7},{7,6},{8,9},{9,8},{10,11... | collective-permute-start | bytes 589832 | tf_op jit(solution)/shard_map/ppermute | solution.py:38
  51.3 3.4 %collective-permute-start.9 = (bf16[2,32,1536]{2,1,0:T(8,128)(2,1)S(1)}, bf16[2,32,1536]{2,1,0:T(8,128)(2,1)S(1)}, u32[]{:S(2)}, u32[]{:S(2)}) collective-permute-start(bf16[2,32,1536]{2,1,0:T(8,128)(2,1)S(1)} %get-tuple-element.86), channel_id=1, source_target_pairs={{0,1},{1,0},{2,3},{3,2},{4,5},{5,4},{6,7},{7,6},{8,9},{9,8},{10,11... | collective-permute-start | bytes 589832 | tf_op jit(solution)/shard_map/ppermute | solution.py:38
  51.4 10.2 %collective-permute-start.11 = (bf16[2,32,1536]{2,1,0:T(8,128)(2,1)S(1)}, bf16[2,32,1536]{2,1,0:T(8,128)(2,1)S(1)}, u32[]{:S(2)}, u32[]{:S(2)}) collective-permute-start(bf16[2,32,1536]{2,1,0:T(8,128)(2,1)S(1)} %add_convert_fusion.8), channel_id=1, source_target_pairs={{0,6},{1,3},{2,0},{3,5},{4,2},{5,7},{6,4},{7,1},{8,14},{9,11},{10,... | collective-permute-start | bytes 589832 | tf_op jit(solution)/shard_map/ppermute | solution.py:38
  52.4 11.3 %collective-permute-start.14 = (bf16[2,32,1536]{2,1,0:T(8,128)(2,1)S(1)}, bf16[2,32,1536]{2,1,0:T(8,128)(2,1)S(1)}, u32[]{:S(2)}, u32[]{:S(2)}) collective-permute-start(bf16[2,32,1536]{2,1,0:T(8,128)(2,1)S(1)} %add_convert_fusion.6), channel_id=1, source_target_pairs={{0,6},{1,3},{2,0},{3,5},{4,2},{5,7},{6,4},{7,1},{8,14},{9,11},{10,... | collective-permute-start | bytes 589832 | tf_op jit(solution)/shard_map/ppermute | solution.py:38
  61.7 6.9 %collective-permute-start.12 = (bf16[2,32,1536]{2,1,0:T(8,128)(2,1)S(1)}, bf16[2,32,1536]{2,1,0:T(8,128)(2,1)S(1)}, u32[]{:S(2)}, u32[]{:S(2)}) collective-permute-start(bf16[2,32,1536]{2,1,0:T(8,128)(2,1)S(1)} %add_convert_fusion.7), channel_id=1, source_target_pairs={{0,6},{1,3},{2,0},{3,5},{4,2},{5,7},{6,4},{7,1},{8,14},{9,11},{10,... | collective-permute-start | bytes 589832 | tf_op jit(solution)/shard_map/ppermute | solution.py:38
  63.8 4.8 %collective-permute-start.15 = (bf16[2,32,1536]{2,1,0:T(8,128)(2,1)S(1)}, bf16[2,32,1536]{2,1,0:T(8,128)(2,1)S(1)}, u32[]{:S(2)}, u32[]{:S(2)}) collective-permute-start(bf16[2,32,1536]{2,1,0:T(8,128)(2,1)S(1)} %add_convert_fusion.5), channel_id=1, source_target_pairs={{0,1},{1,0},{2,3},{3,2},{4,5},{5,4},{6,7},{7,6},{8,9},{9,8},{10,11... | collective-permute-start | bytes 589832 | tf_op jit(solution)/shard_map/ppermute | solution.py:38
  69.5 3.9 %collective-permute-start.16 = (bf16[4,32,1536]{2,1,0:T(8,128)(2,1)S(1)}, bf16[4,32,1536]{2,1,0:T(8,128)(2,1)S(1)}, u32[]{:S(2)}, u32[]{:S(2)}) collective-permute-start(bf16[4,32,1536]{2,1,0:T(8,128)(2,1)S(1)} %get-tuple-element.94.own_b.mids), channel_id=1, source_target_pairs={{0,1},{1,0},{2,3},{3,2},{4,5},{5,4},{6,7},{7,6},{8,9},{9,8},{10,11... | collective-permute-start | bytes 1179656 | tf_op jit(solution)/shard_map/ppermute | solution.py:38
  70.9 18.5 %collective-permute-start.17 = (bf16[4,32,1536]{2,1,0:T(8,128)(2,1)S(1)}, bf16[4,32,1536]{2,1,0:T(8,128)(2,1)S(1)}, u32[]{:S(2)}, u32[]{:S(2)}) collective-permute-start(bf16[4,32,1536]{2,1,0:T(8,128)(2,1)S(1)} %get-tuple-element.94.own_b.mids), channel_id=1, source_target_pairs={{0,2},{1,7},{2,4},{3,1},{4,6},{5,3},{6,0},{7,5},{8,10},{9,15},{10,... | collective-permute-start | bytes 1179656 | tf_op jit(solution)/shard_map/ppermute | solution.py:38
  73.3 20.3 %collective-permute-start.18 = (bf16[4,32,1536]{2,1,0:T(8,128)(2,1)S(1)}, bf16[4,32,1536]{2,1,0:T(8,128)(2,1)S(1)}, u32[]{:S(2)}, u32[]{:S(2)}) collective-permute-start(bf16[4,32,1536]{2,1,0:T(8,128)(2,1)S(1)} %collective-permute-done.16.other), channel_id=1, source_target_pairs={{0,2},{1,7},{2,4},{3,1},{4,6},{5,3},{6,0},{7,5},{8,10},{9,15},{10,... | collective-permute-start | bytes 1179656 | tf_op jit(solution)/shard_map/ppermute | solution.py:38
  89.4 9.6 %collective-permute-start.19 = (bf16[4,32,1536]{2,1,0:T(8,128)(2,1)S(1)}, bf16[4,32,1536]{2,1,0:T(8,128)(2,1)S(1)}, u32[]{:S(2)}, u32[]{:S(2)}) collective-permute-start(bf16[4,32,1536]{2,1,0:T(8,128)(2,1)S(1)} %collective-permute-done.17.near_0), channel_id=1, source_target_pairs={{0,2},{1,7},{2,4},{3,1},{4,6},{5,3},{6,0},{7,5},{8,10},{9,15},{10,... | collective-permute-start | bytes 1179656 | tf_op jit(solution)/shard_map/ppermute | solution.py:38
  93.6 5.4 %collective-permute-start.21 = (bf16[4,32,1536]{2,1,0:T(8,128)(2,1)S(1)}, bf16[4,32,1536]{2,1,0:T(8,128)(2,1)S(1)}, u32[]{:S(2)}, u32[]{:S(2)}) collective-permute-start(bf16[4,32,1536]{2,1,0:T(8,128)(2,1)S(1)} %collective-permute-done.18.near_1), channel_id=1, source_target_pairs={{0,1},{1,0},{2,3},{3,2},{4,5},{5,4},{6,7},{7,6},{8,9},{9,8},{10,11... | collective-permute-start | bytes 1179656 | tf_op jit(solution)/shard_map/ppermute | solution.py:38
  95.5 17.2 %collective-permute-start.24 = (bf16[1920,128]{1,0:T(8,128)(2,1)S(1)}, bf16[1920,128]{1,0:T(8,128)(2,1)S(1)}, u32[]{:S(2)}, u32[]{:S(2)}) collective-permute-start(bf16[1920,128]{1,0:T(8,128)(2,1)S(1)} %pack_new.1), channel_id=1, source_target_pairs={{0,248},{8,240},{16,232},{24,224},{32,216},{40,208},{48,200},{56,1... | collective-permute-start | bytes 1474568 | tf_op jit(solution)/shard_map/ppermute | solution.py:356
  98.2 2.3 %collective-permute-start.20 = (bf16[4,32,1536]{2,1,0:T(8,128)(2,1)S(1)}, bf16[4,32,1536]{2,1,0:T(8,128)(2,1)S(1)}, u32[]{:S(2)}, u32[]{:S(2)}) collective-permute-start(bf16[4,32,1536]{2,1,0:T(8,128)(2,1)S(1)} %collective-permute-done.17.near_0), channel_id=1, source_target_pairs={{0,1},{1,0},{2,3},{3,2},{4,5},{5,4},{6,7},{7,6},{8,9},{9,8},{10,11... | collective-permute-start | bytes 1179656 | tf_op jit(solution)/shard_map/ppermute | solution.py:38
  99.0 2.8 %collective-permute-start.22 = (bf16[4,32,1536]{2,1,0:T(8,128)(2,1)S(1)}, bf16[4,32,1536]{2,1,0:T(8,128)(2,1)S(1)}, u32[]{:S(2)}, u32[]{:S(2)}) collective-permute-start(bf16[4,32,1536]{2,1,0:T(8,128)(2,1)S(1)} %collective-permute-done.19.far), channel_id=1, source_target_pairs={{0,1},{1,0},{2,3},{3,2},{4,5},{5,4},{6,7},{7,6},{8,9},{9,8},{10,11... | collective-permute-start | bytes 1179656 | tf_op jit(solution)/shard_map/ppermute | solution.py:38
  114.6 4.9 %collective-permute-start.30 = (bf16[2,32,1536]{2,1,0:T(8,128)(2,1)S(1)}, bf16[2,32,1536]{2,1,0:T(8,128)(2,1)S(1)}, u32[]{:S(2)}, u32[]{:S(2)}) collective-permute-start(bf16[2,32,1536]{2,1,0:T(8,128)(2,1)S(1)} %get-tuple-element.125), channel_id=1, source_target_pairs={{0,1},{1,0},{2,3},{3,2},{4,5},{5,4},{6,7},{7,6},{8,9},{9,8},{10,11... | collective-permute-start | bytes 589832 | tf_op jit(solution)/shard_map/ppermute | solution.py:38
  115.1 4.4 %collective-permute-start.28 = (f32[2,1536]{1,0:T(2,128)S(1)}, f32[2,1536]{1,0:T(2,128)S(1)}, u32[]{:S(2)}, u32[]{:S(2)}) collective-permute-start(f32[2,1536]{1,0:T(2,128)S(1)} %fusion), channel_id=1, source_target_pairs={{0,2},{1,3},{2,0},{3,1},{4,6},{5,7},{6,4},{7,5},{8,10},{9,11},{10,... | collective-permute-start | bytes 36872 | tf_op jit(solution)/shard_map/ppermute | solution.py:38
  116.1 4.7 %collective-permute-start.23 = (bf16[2,32,1536]{2,1,0:T(8,128)(2,1)S(1)}, bf16[2,32,1536]{2,1,0:T(8,128)(2,1)S(1)}, u32[]{:S(2)}, u32[]{:S(2)}) collective-permute-start(bf16[2,32,1536]{2,1,0:T(8,128)(2,1)S(1)} %get-tuple-element.101), channel_id=1, source_target_pairs={{0,1},{1,0},{2,3},{3,2},{4,5},{5,4},{6,7},{7,6},{8,9},{9,8},{10,11... | collective-permute-start | bytes 589832 | tf_op jit(solution)/shard_map/ppermute | solution.py:38
  116.5 8.3 %collective-permute-start.26 = (bf16[2,32,1536]{2,1,0:T(8,128)(2,1)S(1)}, bf16[2,32,1536]{2,1,0:T(8,128)(2,1)S(1)}, u32[]{:S(2)}, u32[]{:S(2)}) collective-permute-start(bf16[2,32,1536]{2,1,0:T(8,128)(2,1)S(1)} %add_convert_fusion.3), channel_id=1, source_target_pairs={{0,6},{1,3},{2,0},{3,5},{4,2},{5,7},{6,4},{7,1},{8,14},{9,11},{10,... | collective-permute-start | bytes 589832 | tf_op jit(solution)/shard_map/ppermute | solution.py:38
  119.5 9.5 %collective-permute-start.31 = (bf16[2,32,1536]{2,1,0:T(8,128)(2,1)S(1)}, bf16[2,32,1536]{2,1,0:T(8,128)(2,1)S(1)}, u32[]{:S(2)}, u32[]{:S(2)}) collective-permute-start(bf16[2,32,1536]{2,1,0:T(8,128)(2,1)S(1)} %add_convert_fusion.1), channel_id=1, source_target_pairs={{0,6},{1,3},{2,0},{3,5},{4,2},{5,7},{6,4},{7,1},{8,14},{9,11},{10,... | collective-permute-start | bytes 589832 | tf_op jit(solution)/shard_map/ppermute | solution.py:38
  124.9 11.1 %collective-permute-start.29 = (bf16[2,32,1536]{2,1,0:T(8,128)(2,1)S(1)}, bf16[2,32,1536]{2,1,0:T(8,128)(2,1)S(1)}, u32[]{:S(2)}, u32[]{:S(2)}) collective-permute-start(bf16[2,32,1536]{2,1,0:T(8,128)(2,1)S(1)} %add_convert_fusion.2), channel_id=1, source_target_pairs={{0,6},{1,3},{2,0},{3,5},{4,2},{5,7},{6,4},{7,1},{8,14},{9,11},{10,... | collective-permute-start | bytes 589832 | tf_op jit(solution)/shard_map/ppermute | solution.py:38
  129.1 6.9 %collective-permute-start.32 = (bf16[2,32,1536]{2,1,0:T(8,128)(2,1)S(1)}, bf16[2,32,1536]{2,1,0:T(8,128)(2,1)S(1)}, u32[]{:S(2)}, u32[]{:S(2)}) collective-permute-start(bf16[2,32,1536]{2,1,0:T(8,128)(2,1)S(1)} %add_convert_fusion), channel_id=1, source_target_pairs={{0,1},{1,0},{2,3},{3,2},{4,5},{5,4},{6,7},{7,6},{8,9},{9,8},{10,11... | collective-permute-start | bytes 589832 | tf_op jit(solution)/shard_map/ppermute | solution.py:38
  129.2 11.9 %collective-permute-start.36 = (f32[2,1536]{1,0:T(2,128)S(1)}, f32[2,1536]{1,0:T(2,128)S(1)}, u32[]{:S(2)}, u32[]{:S(2)}) collective-permute-start(f32[2,1536]{1,0:T(2,128)S(1)} %add.48), channel_id=1, source_target_pairs={{0,4},{1,5},{2,6},{3,7},{4,0},{5,1},{6,2},{7,3},{8,12},{9,13},{10,... | collective-permute-start | bytes 36872 | tf_op jit(solution)/shard_map/ppermute | solution.py:38
  131.4 18.7 %collective-permute-start.35 = (bf16[2,256,384]{2,1,0:T(8,128)(2,1)S(1)}, bf16[2,256,384]{2,1,0:T(8,128)(2,1)S(1)}, u32[]{:S(2)}, u32[]{:S(2)}) collective-permute-start(bf16[2,256,384]{2,1,0:T(8,128)(2,1)S(1)} %get-tuple-element.129.kept), channel_id=1, source_target_pairs={{0,248},{8,240},{16,232},{24,224},{32,216},{40,208},{48,200},{56,1... | collective-permute-start | bytes 1179656 | tf_op jit(solution)/shard_map/ppermute | solution.py:356
  136.2 10.0 %collective-permute-start.33 = (bf16[32,1536]{1,0:T(8,128)(2,1)S(1)}, bf16[32,1536]{1,0:T(8,128)(2,1)S(1)}, u32[]{:S(2)}, u32[]{:S(2)}) collective-permute-start(bf16[32,1536]{1,0:T(8,128)(2,1)S(1)} %get-tuple-element.126), channel_id=1, source_target_pairs={{0,8},{8,16},{16,24},{24,32},{32,40},{40,48},{48,56},{56,64},{64,7... | collective-permute-start | bytes 294920 | tf_op jit(solution)/shard_map/ppermute | solution.py:351
  139.8 10.2 %collective-permute-start.34 = (bf16[32,1536]{1,0:T(8,128)(2,1)S(1)}, bf16[32,1536]{1,0:T(8,128)(2,1)S(1)}, u32[]{:S(2)}, u32[]{:S(2)}) collective-permute-start(bf16[32,1536]{1,0:T(8,128)(2,1)S(1)} %get-tuple-element.127), channel_id=1, source_target_pairs={{8,0},{16,8},{24,16},{32,24},{40,32},{48,40},{56,48},{64,56},{72,6... | collective-permute-start | bytes 294920 | tf_op jit(solution)/shard_map/ppermute | solution.py:351
  (13 other events, 155.7 us)
